TPU v7x, 32 devices: a whole 2x2x4 slice. The times are simulated.
32 devices in a mesh: dp: 8 (over z, y), grp: 4 (over x, core).
Axes of the slice: x: 2, y: 2, z: 4, core: 2. Of those that a mesh axis runs over, the one named last changes fastest.
Arguments:
- states: bfloat16 [4096, 2048], P(('dp', 'grp')), may hold values from -60 to 60
- projection: bfloat16 [2048, 768], replicated, may hold values from -0.125 to 0.125
- owner_group: int32 [4096, 1], P(('dp', 'grp')), may hold values from 0 to 7; in each aligned block of 128 rows (0 to 127, 128 to 255, ...) at most 32 rows name the same one
- cluster_sub: int32 [4096], P(('dp', 'grp')), may hold values from 0 to 3
- priority: int32 [4096], P(('dp', 'grp')), may hold values from 0 to 4095, each once
Outputs:
- dup_score: float32 [4096], P(('dp', 'grp'))
Inputs may be any that keep to these rules, and one draw needn't show every extreme that they name: `owner_group`: in each aligned block of 128 rows (the rows of one device) no owner is named by more than 32 rows; in some block some owner is named by exactly 32 rows.
All inputs are finite; a program needn't handle non-finite values.
Results may differ from a plain program's by a relative error of at most 0.0012.
Values may be sent and summed in bfloat16 or wider, within the bound.
No kernel may reach another device: no remote copies, remote signals or barrier semaphores. Data moves between devices by JAX's collectives and lax.ppermute only.
A program may use at most 64 MiB of HBM per device.

v0:
```python
import math

import jax
import jax.numpy as jnp
from jax import lax
from jax.experimental import pallas as pl
from jax.experimental.pallas import tpu as pltpu
from jax.sharding import Mesh, PartitionSpec as P

AXES = ("line", "mid", "grp")
NOTE_ROWS = 8
RADIX = 256
CHUNKS = 4
VMEM = pl.BlockSpec(memory_space=pltpu.VMEM)
HBM = pl.BlockSpec(memory_space=pltpu.HBM)


def embed_kernel(
    states_hbm, proj_hbm, owner_hbm, sub_hbm, prio_hbm, block_ref,
    states, proj, owner, sub, prio, big_sem, small_sem,
):
    rows, depth = states.shape
    width = proj.shape[1]
    span = depth // CHUNKS
    copies = []
    for i in range(CHUNKS):
        part = pl.ds(i * span, span)
        pair = (
            pltpu.make_async_copy(states_hbm.at[:, part], states.at[:, part], big_sem.at[0, i]),
            pltpu.make_async_copy(proj_hbm.at[part], proj.at[part], big_sem.at[1, i]),
        )
        copies.append(pair)
        for copy in pair:
            copy.start()
    small = [
        pltpu.make_async_copy(src, dst, small_sem.at[i])
        for i, (src, dst) in enumerate(((owner_hbm, owner), (sub_hbm, sub), (prio_hbm, prio)))
    ]
    for copy in small:
        copy.start()
    projected = None
    for i, pair in enumerate(copies):
        for copy in pair:
            copy.wait()
        part = slice(i * span, (i + 1) * span)
        term = jnp.dot(states[:, part], proj[part, :], preferred_element_type=jnp.float32)
        projected = term if projected is None else projected + term
    square_sum = jnp.sum(projected * projected, axis=1, keepdims=True)
    embedding = projected * lax.rsqrt(square_sum + 1e-06)
    for copy in small:
        copy.wait()
    rank = prio[...]
    high = lax.shift_right_logical(rank, 8)
    fields = (owner[...] + 1, sub[...], high, rank - high * RADIX)
    notes = [jnp.broadcast_to(f.astype(jnp.float32), (NOTE_ROWS, rows)) for f in fields]
    notes.append(jnp.zeros((NOTE_ROWS, width - len(fields) * rows), jnp.float32))
    block = jnp.concatenate([embedding, jnp.concatenate(notes, axis=1)], axis=0)
    block_ref[...] = block.astype(jnp.bfloat16)


def embed(states, projection, owner, sub, prio):
    rows, depth = states.shape
    width = projection.shape[1]
    return pl.pallas_call(
        embed_kernel,
        in_specs=[HBM] * 5,
        out_specs=VMEM,
        out_shape=jax.ShapeDtypeStruct((rows + NOTE_ROWS, width), jnp.bfloat16),
        scratch_shapes=[
            pltpu.VMEM((rows, depth), jnp.bfloat16),
            pltpu.VMEM((depth, width), jnp.bfloat16),
            pltpu.VMEM((1, rows), jnp.int32),
            pltpu.VMEM((1, rows), jnp.int32),
            pltpu.VMEM((1, rows), jnp.int32),
            pltpu.SemaphoreType.DMA((2, CHUNKS)),
            pltpu.SemaphoreType.DMA((3,)),
        ],
        compiler_params=pltpu.CompilerParams(vmem_limit_bytes=60 << 20),
        name="embed",
    )(states, projection, owner, sub, prio)


def read_notes(ref, rows):
    tail = ref[rows:, :].astype(jnp.float32)
    owner, sub, high, low = (tail[:1, i * rows:(i + 1) * rows] for i in range(4))
    return (owner - 1.0) * 4.0 + sub, high * float(RADIX) + low


def score_kernel(row_count, lane_count, has_lines, has_backs, hold, *refs):
    refs = list(refs)
    row_refs = [refs.pop(0) for _ in range(row_count)]
    lane_refs = [refs.pop(0) for _ in range(lane_count)]
    seen_lines = refs.pop(0) if has_lines else None
    seen_backs = [refs.pop(0) for _ in range(row_count)] if has_backs else None
    lines_out, *back_outs = refs[:1 + row_count]
    rows = lines_out.shape[1]
    if hold:
        refs[-1][...] = row_refs[0][...]
    row_notes = [read_notes(ref, rows) for ref in row_refs]
    lane_notes = [read_notes(ref, rows) for ref in lane_refs]
    fill = jnp.zeros((-2 * row_count % 8, rows), jnp.float32)
    lines = [line for pair in row_notes for line in pair]
    columns = jnp.concatenate(lines + ([fill] if fill.size else []), axis=0).T
    cosine = lax.dot_general(
        jnp.concatenate([ref[:rows, :] for ref in row_refs], axis=0),
        jnp.concatenate([ref[:rows, :] for ref in lane_refs], axis=0),
        (((1,), (1,)), ((), ())),
        preferred_element_type=jnp.float32,
    )
    best = [jnp.full((rows, rows), -1.0, jnp.float32)] * lane_count
    table = jnp.full((rows, rows), -1.0, jnp.float32)
    lane_ids = lax.broadcasted_iota(jnp.int32, (rows, rows), 1)
    for i in range(row_count):
        row_cluster, row_prio = columns[:, 2 * i:2 * i + 1], columns[:, 2 * i + 1:2 * i + 2]
        back = jnp.full((rows, rows), -1.0, jnp.float32)
        for j, (lane_cluster, lane_prio) in enumerate(lane_notes):
            here = cosine[i * rows:(i + 1) * rows, j * rows:(j + 1) * rows]
            same = jnp.where(row_cluster == lane_cluster, here, -1.0)
            earlier = row_prio < lane_prio
            best[j] = jnp.maximum(best[j], jnp.where(earlier, same, -1.0))
            if j > 0:
                back = jnp.maximum(back, jnp.where(earlier, -1.0, same))
        table = jnp.where(lane_ids == i, jnp.max(back, axis=1, keepdims=True), table)
    table = table.T
    for i, ref in enumerate(back_outs):
        line = table[i:i + 1]
        ref[...] = jnp.maximum(line, seen_backs[i][...]) if has_backs else line
    lines = jnp.concatenate([jnp.max(b, axis=0, keepdims=True) for b in best], axis=0)
    lines_out[...] = jnp.maximum(lines, seen_lines[...]) if has_lines else lines


def score(name, row_blocks, lane_blocks, lines=(), backs=(), hold=False):
    high, width = row_blocks[0].shape
    rows = high - NOTE_ROWS
    inputs = [*row_blocks, *lane_blocks, *lines, *backs]
    shapes = [(len(lane_blocks), rows)] + [(1, rows)] * len(row_blocks)
    outs = [jax.ShapeDtypeStruct(shape, jnp.float32) for shape in shapes]
    if hold:
        outs.append(jax.ShapeDtypeStruct((high, width), row_blocks[0].dtype))
    counts = len(row_blocks), len(lane_blocks)
    flags = len(lines) > 0, len(backs) > 0, hold
    return pl.pallas_call(
        lambda *refs: score_kernel(*counts, *flags, *refs),
        in_specs=[VMEM] * len(inputs),
        out_specs=[VMEM] * len(outs),
        out_shape=outs,
        compiler_params=pltpu.CompilerParams(vmem_limit_bytes=48 << 20),
        cost_estimate=pl.CostEstimate(
            flops=2 * math.prod(counts) * rows * rows * width,
            bytes_accessed=2 * sum(counts) * rows * width,
            transcendentals=0,
        ),
        name=name,
    )(*inputs)


def tournament(line):
    moves = [[(i, (i + s) % line) for i in range(line)] for s in range(1, (line + 1) // 2)]
    if line % 2 == 0:
        half = line // 2
        pairs = [(i, i + half) if i % 2 else (i + half, i) for i in range(half)]
        sent, met = {a for a, _ in pairs}, {b for _, b in pairs}
        idle = [i for i in range(line) if i not in sent]
        free = [i for i in range(line) if i not in met]
        moves.append(pairs + list(zip(idle, free)))
    return moves


def on_device(states, projection, owner_group, cluster_sub, priority):
    line, grp = lax.axis_size("line"), lax.axis_size("grp")
    plane = lax.axis_size("mid") * grp
    rows = states.shape[0]

    def move(array, pairs):
        whole = [(a * plane + p, b * plane + p) for a, b in pairs for p in range(plane)]
        return lax.ppermute(array, AXES, whole)

    def swap(array, step):
        pairs = [(i, i // plane * plane + (i % plane ^ step)) for i in range(line * plane)]
        return lax.ppermute(array, AXES, pairs)

    block = embed(
        states,
        projection,
        owner_group.reshape(1, rows),
        cluster_sub.reshape(1, rows),
        priority.reshape(1, rows),
    )
    moves = tournament(line)
    visitors = [move(block, pairs) for pairs in moves]
    steps = range(2, plane, 2)
    plane_blocks = [swap(block, step) for step in steps]

    soon, last = plane_blocks[:-2], plane_blocks[-2:]
    lines, *backs, held = score("score_soon", [block] + soon, [block] + visitors, hold=True)
    lanes = [held] + visitors
    lines, *more = score("score_late", last, lanes, lines=[lines])
    lanes = [swap(block, 1)] + [swap(visitor, 1) for visitor in visitors]
    theirs, own_back, *backs = score(
        "score_partner", [held] + soon + last, lanes, backs=backs + more
    )
    lines = jnp.maximum(lines, swap(theirs, 1))
    total = jnp.maximum(lines[:1], own_back)
    for step, back in zip(steps, backs):
        total = jnp.maximum(total, swap(back, step))
    for i, pairs in enumerate(moves):
        total = jnp.maximum(total, move(lines[i + 1:i + 2], [(b, a) for a, b in pairs]))
    return total.reshape(rows)


def solution(mesh):
    num_dp, num_grp = mesh.shape["dp"], mesh.shape["grp"]
    line = min(num_dp, 1 << (int(math.log2(num_dp * num_grp)) // 2))
    split = Mesh(mesh.devices.reshape(line, num_dp // line, num_grp), AXES)
    in_specs = (P(AXES, None), P(), P(AXES, None), P(AXES), P(AXES))
    return jax.shard_map(
        on_device, mesh=split, in_specs=in_specs, out_specs=P(AXES), check_vma=False
    )
```

profile of v0, /device:TPU:0, one launch (start us, length us, event | category | flops | bytes accessed | tf_op | source)
XLA Modules:
  0.0 31.7 jit_solution(4395133186236551049)
XLA Ops:
  0.0 3.3 %embed.1.refs_0_.refs_2_ = bf16[136,768]{1,0:T(8,128)(2,1)} custom-call(bf16[128,2048]{1,0:T(8,128)(2,1)} %states_hbm.1, bf16[2048,768]{1,0:T(8,128)(2,1)} %proj_hbm.1, s32[1,128]{1,0:T(1,128)} %bitcast.5, s32[1,128]{1,0:T(1,128)} %bitcast.6, s32[1,128]{1,0:T(1,128)} %bitcast.7), custom_call_target="tpu_custom_call" | custom-call | tf_op jit(solution)/shard_map/embed/pallas_call | solution.py:64
  3.3 3.1 %collective-permute-start.3 = (bf16[136,768]{1,0:T(8,128)(2,1)}, bf16[136,768]{1,0:T(8,128)(2,1)S(1)}, u32[]{:S(2)}, u32[]{:S(2)}) collective-permute-start(bf16[136,768]{1,0:T(8,128)(2,1)} %embed.1.refs_0_.refs_2_), channel_id=1, source_target_pairs={{0,8},{1,9},{2,10},{3,11},{4,12},{5,13},{6,14},{7,15},{8,16},{9,17... | collective-permute-start | bytes 626696 | tf_op jit(solution)/shard_map/ppermute | solution.py:176
  6.3 1.6 %collective-permute-start.4 = (bf16[136,768]{1,0:T(8,128)(2,1)}, bf16[136,768]{1,0:T(8,128)(2,1)S(1)}, u32[]{:S(2)}, u32[]{:S(2)}) collective-permute-start(bf16[136,768]{1,0:T(8,128)(2,1)} %embed.1.refs_0_.refs_2_), channel_id=1, source_target_pairs={{16,0},{17,1},{18,2},{19,3},{20,4},{21,5},{22,6},{23,7},{8,24},{9,... | collective-permute-start | bytes 626696 | tf_op jit(solution)/shard_map/ppermute | solution.py:176
  7.9 1.5 %collective-permute-start.2 = (bf16[136,768]{1,0:T(8,128)(2,1)}, bf16[136,768]{1,0:T(8,128)(2,1)S(1)}, u32[]{:S(2)}, u32[]{:S(2)}) collective-permute-start(bf16[136,768]{1,0:T(8,128)(2,1)} %embed.1.refs_0_.refs_2_), channel_id=1, source_target_pairs={{0,2},{1,3},{2,0},{3,1},{4,6},{5,7},{6,4},{7,5},{8,10},{9,11},{10,... | collective-permute-start | bytes 626696 | tf_op jit(solution)/shard_map/ppermute | solution.py:180
  9.4 1.5 %collective-permute-start = (bf16[136,768]{1,0:T(8,128)(2,1)}, bf16[136,768]{1,0:T(8,128)(2,1)S(1)}, u32[]{:S(2)}, u32[]{:S(2)}) collective-permute-start(bf16[136,768]{1,0:T(8,128)(2,1)} %embed.1.refs_0_.refs_2_), channel_id=1, source_target_pairs={{0,4},{1,5},{2,6},{3,7},{4,0},{5,1},{6,2},{7,3},{8,12},{9,13},{10,... | collective-permute-start | bytes 626696 | tf_op jit(solution)/shard_map/ppermute | solution.py:180
  10.9 0.5 %collective-permute-start.1 = (bf16[136,768]{1,0:T(8,128)(2,1)}, bf16[136,768]{1,0:T(8,128)(2,1)S(1)}, u32[]{:S(2)}, u32[]{:S(2)}) collective-permute-start(bf16[136,768]{1,0:T(8,128)(2,1)} %embed.1.refs_0_.refs_2_), channel_id=1, source_target_pairs={{0,6},{1,7},{2,4},{3,5},{4,2},{5,3},{6,0},{7,1},{8,14},{9,15},{10,... | collective-permute-start | bytes 626696 | tf_op jit(solution)/shard_map/ppermute | solution.py:180
  11.4 3.2 %collective-permute-done.3.refs_3_ = bf16[136,768]{1,0:T(8,128)(2,1)S(1)} collective-permute-done((bf16[136,768]{1,0:T(8,128)(2,1)}, bf16[136,768]{1,0:T(8,128)(2,1)S(1)}, u32[]{:S(2)}, u32[]{:S(2)}) %collective-permute-start.3) | collective-permute-done | bytes 208928 | tf_op jit(solution)/shard_map/ppermute | solution.py:176
  14.6 3.6 %collective-permute-done.4.refs_4_ = bf16[136,768]{1,0:T(8,128)(2,1)S(1)} collective-permute-done((bf16[136,768]{1,0:T(8,128)(2,1)}, bf16[136,768]{1,0:T(8,128)(2,1)S(1)}, u32[]{:S(2)}, u32[]{:S(2)}) %collective-permute-start.4) | collective-permute-done | bytes 208928 | tf_op jit(solution)/shard_map/ppermute | solution.py:176
  18.2 0.0 collective-permute-start.6
  18.2 0.5 %collective-permute-start.7 = (bf16[136,768]{1,0:T(8,128)(2,1)S(1)}, bf16[136,768]{1,0:T(8,128)(2,1)S(1)}, u32[]{:S(2)}, u32[]{:S(2)}) collective-permute-start(bf16[136,768]{1,0:T(8,128)(2,1)S(1)} %collective-permute-done.4.refs_4_), channel_id=1, source_target_pairs={{0,1},{1,0},{2,3},{3,2},{4,5},{5,4},{6,7},{7,6},{8,9},{9,8},{10,11... | collective-permute-start | bytes 626696 | tf_op jit(solution)/shard_map/ppermute | solution.py:180
  18.7 0.9 %copy-done = bf16[136,768]{1,0:T(8,128)(2,1)S(1)} copy-done((bf16[136,768]{1,0:T(8,128)(2,1)S(1)}, bf16[136,768]{1,0:T(8,128)(2,1)}, u32[]{:S(2)}) %copy-start) | copy-done | bytes 208920
  19.7 0.5 %score_soon.1 = (f32[3,128]{1,0:T(4,128)S(1)}, f32[1,128]{1,0:T(1,128)S(1)}, f32[1,128]{1,0:T(1,128)S(1)}, bf16[136,768]{1,0:T(8,128)(2,1)S(1)}) custom-call(bf16[136,768]{1,0:T(8,128)(2,1)S(1)} %copy-done, bf16[136,768]{1,0:T(8,128)(2,1)S(1)} %collective-permute-done.2.refs_1_, bf16[136,768]{1,0:T(8,128)(2,1)S(1)} %copy-done, ...), custom_call_target="tpu_custom_call" | custom-call | flops 150994944 | bytes 983040 | tf_op jit(solution)/shard_map/score_soon/pallas_call | solution.py:142
  20.2 0.6 %score_late.1 = (f32[3,128]{1,0:T(4,128)S(1)}, f32[1,128]{1,0:T(1,128)S(1)}, f32[1,128]{1,0:T(1,128)S(1)}) custom-call(bf16[136,768]{1,0:T(8,128)(2,1)S(1)} %collective-permute-done.refs_0_.refs_2_, bf16[136,768]{1,0:T(8,128)(2,1)S(1)} %collective-permute-done.1.refs_1_.refs_3_, bf16[136,768]{1,0:T(8,128)(2,1)S(1)} %get-tuple-element.17.refs_2_.refs_0_, ...), custom_call_target="tpu_custom_call" | custom-call | flops 150994944 | bytes 983040 | tf_op jit(solution)/shard_map/score_late/pallas_call | solution.py:142
  20.8 0.8 %score_partner.1 = (f32[3,128]{1,0:T(4,128)S(1)}, f32[1,128]{1,0:T(1,128)S(1)}, f32[1,128]{1,0:T(1,128)S(1)}, f32[1,128]{1,0:T(1,128)S(1)}, f32[1,128]{1,0:T(1,128)S(1)}) custom-call(bf16[136,768]{1,0:T(8,128)(2,1)S(1)} %get-tuple-element.17.refs_2_.refs_0_, bf16[136,768]{1,0:T(8,128)(2,1)S(1)} %collective-permute-done.2.refs_1_, ...), custom_call_target="tpu_custom_call" | custom-call | flops 301989888 | bytes 1376256 | tf_op jit(solution)/shard_map/score_partner/pallas_call | solution.py:142
  21.5 0.1 collective-permute-start.8
  21.6 1.6 %collective-permute-start.10 = (f32[1,128]{1,0:T(1,128)S(1)}, f32[1,128]{1,0:T(1,128)S(1)}, u32[]{:S(2)}, u32[]{:S(2)}) collective-permute-start(f32[1,128]{1,0:T(1,128)S(1)} %get-tuple-element.27), channel_id=1, source_target_pairs={{0,4},{1,5},{2,6},{3,7},{4,0},{5,1},{6,2},{7,3},{8,12},{9,13},{10,... | collective-permute-start | bytes 1544 | tf_op jit(solution)/shard_map/ppermute | solution.py:180
  23.2 1.4 %collective-permute-start.11 = (f32[1,128]{1,0:T(1,128)S(1)}, f32[1,128]{1,0:T(1,128)S(1)}, u32[]{:S(2)}, u32[]{:S(2)}) collective-permute-start(f32[1,128]{1,0:T(1,128)S(1)} %get-tuple-element.28), channel_id=1, source_target_pairs={{0,6},{1,7},{2,4},{3,5},{4,2},{5,3},{6,0},{7,1},{8,14},{9,15},{10,... | collective-permute-start | bytes 1544 | tf_op jit(solution)/shard_map/ppermute | solution.py:180
  24.6 0.5 %collective-permute-start.9 = (f32[1,128]{1,0:T(1,128)S(1)}, f32[1,128]{1,0:T(1,128)S(1)}, u32[]{:S(2)}, u32[]{:S(2)}) collective-permute-start(f32[1,128]{1,0:T(1,128)S(1)} %get-tuple-element.26), channel_id=1, source_target_pairs={{0,2},{1,3},{2,0},{3,1},{4,6},{5,7},{6,4},{7,5},{8,10},{9,11},{10,... | collective-permute-start | bytes 1544 | tf_op jit(solution)/shard_map/ppermute | solution.py:180
  25.2 2.5 %collective-permute-start.12 = (f32[1,128]{1,0:T(1,128)S(1)}, f32[1,128]{1,0:T(1,128)S(1)}, u32[]{:S(2)}, u32[]{:S(2)}) collective-permute-start(f32[1,128]{1,0:T(1,128)S(1)} %get-tuple-element.29), channel_id=1, source_target_pairs={{8,0},{9,1},{10,2},{11,3},{12,4},{13,5},{14,6},{15,7},{16,8},{17,9... | collective-permute-start | bytes 1544 | tf_op jit(solution)/shard_map/ppermute | solution.py:176
  27.7 0.3 %collective-permute-start.13 = (f32[1,128]{1,0:T(1,128)S(1)}, f32[1,128]{1,0:T(1,128)S(1)}, u32[]{:S(2)}, u32[]{:S(2)}) collective-permute-start(f32[1,128]{1,0:T(1,128)S(1)} %get-tuple-element.30), channel_id=1, source_target_pairs={{0,16},{1,17},{2,18},{3,19},{4,20},{5,21},{6,22},{7,23},{24,8},{25... | collective-permute-start | bytes 1544 | tf_op jit(solution)/shard_map/ppermute | solution.py:176
  28.0 0.2 collective-permute-done.9
  28.2 0.8 %collective-permute-done.12 = f32[1,128]{1,0:T(1,128)S(1)} collective-permute-done((f32[1,128]{1,0:T(1,128)S(1)}, f32[1,128]{1,0:T(1,128)S(1)}, u32[]{:S(2)}, u32[]{:S(2)}) %collective-permute-start.12) | collective-permute-done | bytes 544 | tf_op jit(solution)/shard_map/ppermute | solution.py:176
  29.0 2.2 %collective-permute-done.13 = f32[1,128]{1,0:T(1,128)S(1)} collective-permute-done((f32[1,128]{1,0:T(1,128)S(1)}, f32[1,128]{1,0:T(1,128)S(1)}, u32[]{:S(2)}, u32[]{:S(2)}) %collective-permute-start.13) | collective-permute-done | bytes 544 | tf_op jit(solution)/shard_map/ppermute | solution.py:176
  31.2 0.5 %maximum_bitcast_fusion = f32[128]{0:T(128)} fusion(f32[1,128]{1,0:T(1,128)S(1)} %collective-permute-done.13, f32[1,128]{1,0:T(1,128)S(1)} %collective-permute-done.12, f32[1,128]{1,0:T(1,128)S(1)} %collective-permute-done.11, f32[1,128]{1,0:T(1,128)S(1)} %collective-permute-done.10, f32[1,128]{1,0:T(1,128)S(1)} %collective-permute-done.9, ...), kind=kLoop, calls=%fused_computation | loop fusion | flops 768 | bytes 4096 | tf_op jit(solution)/shard_map/reshape | solution.py:208
  (13 shorter events, 0.0 us)
Async XLA Ops:
  3.3 11.4 %collective-permute-start.3 = (bf16[136,768]{1,0:T(8,128)(2,1)}, bf16[136,768]{1,0:T(8,128)(2,1)S(1)}, u32[]{:S(2)}, u32[]{:S(2)}) collective-permute-start(bf16[136,768]{1,0:T(8,128)(2,1)} %embed.1.refs_0_.refs_2_), channel_id=1, source_target_pairs={{0,8},{1,9},{2,10},{3,11},{4,12},{5,13},{6,14},{7,15},{8,16},{9,17... | collective-permute-start | bytes 626696 | tf_op jit(solution)/shard_map/ppermute | solution.py:176
  6.3 11.9 %collective-permute-start.4 = (bf16[136,768]{1,0:T(8,128)(2,1)}, bf16[136,768]{1,0:T(8,128)(2,1)S(1)}, u32[]{:S(2)}, u32[]{:S(2)}) collective-permute-start(bf16[136,768]{1,0:T(8,128)(2,1)} %embed.1.refs_0_.refs_2_), channel_id=1, source_target_pairs={{16,0},{17,1},{18,2},{19,3},{20,4},{21,5},{22,6},{23,7},{8,24},{9,... | collective-permute-start | bytes 626696 | tf_op jit(solution)/shard_map/ppermute | solution.py:176
  7.9 10.3 %collective-permute-start.2 = (bf16[136,768]{1,0:T(8,128)(2,1)}, bf16[136,768]{1,0:T(8,128)(2,1)S(1)}, u32[]{:S(2)}, u32[]{:S(2)}) collective-permute-start(bf16[136,768]{1,0:T(8,128)(2,1)} %embed.1.refs_0_.refs_2_), channel_id=1, source_target_pairs={{0,2},{1,3},{2,0},{3,1},{4,6},{5,7},{6,4},{7,5},{8,10},{9,11},{10,... | collective-permute-start | bytes 626696 | tf_op jit(solution)/shard_map/ppermute | solution.py:180
  9.4 10.8 %collective-permute-start = (bf16[136,768]{1,0:T(8,128)(2,1)}, bf16[136,768]{1,0:T(8,128)(2,1)S(1)}, u32[]{:S(2)}, u32[]{:S(2)}) collective-permute-start(bf16[136,768]{1,0:T(8,128)(2,1)} %embed.1.refs_0_.refs_2_), channel_id=1, source_target_pairs={{0,4},{1,5},{2,6},{3,7},{4,0},{5,1},{6,2},{7,3},{8,12},{9,13},{10,... | collective-permute-start | bytes 626696 | tf_op jit(solution)/shard_map/ppermute | solution.py:180
  10.9 9.3 %collective-permute-start.1 = (bf16[136,768]{1,0:T(8,128)(2,1)}, bf16[136,768]{1,0:T(8,128)(2,1)S(1)}, u32[]{:S(2)}, u32[]{:S(2)}) collective-permute-start(bf16[136,768]{1,0:T(8,128)(2,1)} %embed.1.refs_0_.refs_2_), channel_id=1, source_target_pairs={{0,6},{1,7},{2,4},{3,5},{4,2},{5,3},{6,0},{7,1},{8,14},{9,15},{10,... | collective-permute-start | bytes 626696 | tf_op jit(solution)/shard_map/ppermute | solution.py:180
  14.6 6.2 %collective-permute-start.5 = (bf16[136,768]{1,0:T(8,128)(2,1)}, bf16[136,768]{1,0:T(8,128)(2,1)S(1)}, u32[]{:S(2)}, u32[]{:S(2)}) collective-permute-start(bf16[136,768]{1,0:T(8,128)(2,1)} %embed.1.refs_0_.refs_2_), channel_id=1, source_target_pairs={{0,1},{1,0},{2,3},{3,2},{4,5},{5,4},{6,7},{7,6},{8,9},{9,8},{10,11... | collective-permute-start | bytes 626696 | tf_op jit(solution)/shard_map/ppermute | solution.py:180
  18.2 2.6 %collective-permute-start.6 = (bf16[136,768]{1,0:T(8,128)(2,1)S(1)}, bf16[136,768]{1,0:T(8,128)(2,1)S(1)}, u32[]{:S(2)}, u32[]{:S(2)}) collective-permute-start(bf16[136,768]{1,0:T(8,128)(2,1)S(1)} %collective-permute-done.3.refs_3_), channel_id=1, source_target_pairs={{0,1},{1,0},{2,3},{3,2},{4,5},{5,4},{6,7},{7,6},{8,9},{9,8},{10,11... | collective-permute-start | bytes 626696 | tf_op jit(solution)/shard_map/ppermute | solution.py:180
  18.2 2.5 %collective-permute-start.7 = (bf16[136,768]{1,0:T(8,128)(2,1)S(1)}, bf16[136,768]{1,0:T(8,128)(2,1)S(1)}, u32[]{:S(2)}, u32[]{:S(2)}) collective-permute-start(bf16[136,768]{1,0:T(8,128)(2,1)S(1)} %collective-permute-done.4.refs_4_), channel_id=1, source_target_pairs={{0,1},{1,0},{2,3},{3,2},{4,5},{5,4},{6,7},{7,6},{8,9},{9,8},{10,11... | collective-permute-start | bytes 626696 | tf_op jit(solution)/shard_map/ppermute | solution.py:180
  18.7 0.9 %copy-start = (bf16[136,768]{1,0:T(8,128)(2,1)S(1)}, bf16[136,768]{1,0:T(8,128)(2,1)}, u32[]{:S(2)}) copy-start(bf16[136,768]{1,0:T(8,128)(2,1)} %embed.1.refs_0_.refs_2_) | copy-start | bytes 626692
  21.5 3.6 %collective-permute-start.8 = (f32[3,128]{1,0:T(4,128)S(1)}, f32[3,128]{1,0:T(4,128)S(1)}, u32[]{:S(2)}, u32[]{:S(2)}) collective-permute-start(f32[3,128]{1,0:T(4,128)S(1)} %get-tuple-element.24), channel_id=1, source_target_pairs={{0,1},{1,0},{2,3},{3,2},{4,5},{5,4},{6,7},{7,6},{8,9},{9,8},{10,11... | collective-permute-start | bytes 4616 | tf_op jit(solution)/shard_map/ppermute | solution.py:180
  21.6 6.4 %collective-permute-start.10 = (f32[1,128]{1,0:T(1,128)S(1)}, f32[1,128]{1,0:T(1,128)S(1)}, u32[]{:S(2)}, u32[]{:S(2)}) collective-permute-start(f32[1,128]{1,0:T(1,128)S(1)} %get-tuple-element.27), channel_id=1, source_target_pairs={{0,4},{1,5},{2,6},{3,7},{4,0},{5,1},{6,2},{7,3},{8,12},{9,13},{10,... | collective-permute-start | bytes 1544 | tf_op jit(solution)/shard_map/ppermute | solution.py:180
  23.2 4.8 %collective-permute-start.11 = (f32[1,128]{1,0:T(1,128)S(1)}, f32[1,128]{1,0:T(1,128)S(1)}, u32[]{:S(2)}, u32[]{:S(2)}) collective-permute-start(f32[1,128]{1,0:T(1,128)S(1)} %get-tuple-element.28), channel_id=1, source_target_pairs={{0,6},{1,7},{2,4},{3,5},{4,2},{5,3},{6,0},{7,1},{8,14},{9,15},{10,... | collective-permute-start | bytes 1544 | tf_op jit(solution)/shard_map/ppermute | solution.py:180
  24.6 3.5 %collective-permute-start.9 = (f32[1,128]{1,0:T(1,128)S(1)}, f32[1,128]{1,0:T(1,128)S(1)}, u32[]{:S(2)}, u32[]{:S(2)}) collective-permute-start(f32[1,128]{1,0:T(1,128)S(1)} %get-tuple-element.26), channel_id=1, source_target_pairs={{0,2},{1,3},{2,0},{3,1},{4,6},{5,7},{6,4},{7,5},{8,10},{9,11},{10,... | collective-permute-start | bytes 1544 | tf_op jit(solution)/shard_map/ppermute | solution.py:180
  25.2 3.8 %collective-permute-start.12 = (f32[1,128]{1,0:T(1,128)S(1)}, f32[1,128]{1,0:T(1,128)S(1)}, u32[]{:S(2)}, u32[]{:S(2)}) collective-permute-start(f32[1,128]{1,0:T(1,128)S(1)} %get-tuple-element.29), channel_id=1, source_target_pairs={{8,0},{9,1},{10,2},{11,3},{12,4},{13,5},{14,6},{15,7},{16,8},{17,9... | collective-permute-start | bytes 1544 | tf_op jit(solution)/shard_map/ppermute | solution.py:176
  27.7 3.5 %collective-permute-start.13 = (f32[1,128]{1,0:T(1,128)S(1)}, f32[1,128]{1,0:T(1,128)S(1)}, u32[]{:S(2)}, u32[]{:S(2)}) collective-permute-start(f32[1,128]{1,0:T(1,128)S(1)} %get-tuple-element.30), channel_id=1, source_target_pairs={{0,16},{1,17},{2,18},{3,19},{4,20},{5,21},{6,22},{7,23},{24,8},{25... | collective-permute-start | bytes 1544 | tf_op jit(solution)/shard_map/ppermute | solution.py:176
where the time goes:
time: 31.9 us; the launch traced here: 31.7 us
  starting transfers between devices  15.1 us (47%)
  waiting for transfers between devices  10 us (31%)
  Pallas kernels  5.1 us (16%)
  local copies, waits for them, and re-layouts  0.94 us (3%)
  other arithmetic  0.52 us (2%)
    ppermute x4, waiting for transfers between devices, move(): return lax.ppermute(array, AXES, whole)  9.83 us
    ppermute x10, starting transfers between devices, swap(): return lax.ppermute(array, AXES, pairs)  7.63 us
    ppermute x4, starting transfers between devices, move(): return lax.ppermute(array, AXES, whole)  7.47 us
    pallas_call x1, Pallas kernels, embed(): pl.pallas_call(embed_kernel, in_specs=[HBM] * 5, out_specs=VMEM, out_shap...  3.26 us
    pallas_call x3, Pallas kernels, score(): pl.pallas_call(lambda *refs: score_kernel(*counts, *flags, *refs), in_spe...  1.84 us
    unnamed x2, local copies, waits for them, and re-layouts  0.93 us
  transfers between devices with their start and end apart: 14, of which 5 were waited for; matrix products, arithmetic and copies ran while one was open for 0% of the time, Pallas kernels for 3%

commit v1 on v0

--- a/solution.py
+++ b/solution.py
@@ -10,7 +10,7 @@
 AXES = ("line", "mid", "grp")
 NOTE_ROWS = 8
 RADIX = 256
-CHUNKS = 4
+CHUNKS = 8
 VMEM = pl.BlockSpec(memory_space=pltpu.VMEM)
 HBM = pl.BlockSpec(memory_space=pltpu.HBM)
 
@@ -86,13 +86,13 @@
     return (owner - 1.0) * 4.0 + sub, high * float(RADIX) + low
 
 
-def score_kernel(row_count, lane_count, has_lines, has_backs, hold, *refs):
+def score_kernel(row_count, lane_count, products, back_rows, has_lines, seen_rows, hold, *refs):
     refs = list(refs)
     row_refs = [refs.pop(0) for _ in range(row_count)]
     lane_refs = [refs.pop(0) for _ in range(lane_count)]
     seen_lines = refs.pop(0) if has_lines else None
-    seen_backs = [refs.pop(0) for _ in range(row_count)] if has_backs else None
-    lines_out, *back_outs = refs[:1 + row_count]
+    seen_backs = {i: refs.pop(0) for i in seen_rows}
+    lines_out = refs.pop(0)
     rows = lines_out.shape[1]
     if hold:
         refs[-1][...] = row_refs[0][...]
@@ -101,61 +101,71 @@
     fill = jnp.zeros((-2 * row_count % 8, rows), jnp.float32)
     lines = [line for pair in row_notes for line in pair]
     columns = jnp.concatenate(lines + ([fill] if fill.size else []), axis=0).T
-    cosine = lax.dot_general(
-        jnp.concatenate([ref[:rows, :] for ref in row_refs], axis=0),
-        jnp.concatenate([ref[:rows, :] for ref in lane_refs], axis=0),
-        (((1,), (1,)), ((), ())),
-        preferred_element_type=jnp.float32,
-    )
-    best = [jnp.full((rows, rows), -1.0, jnp.float32)] * lane_count
+    best, back = [None] * lane_count, [None] * row_count
+
+    def top(old, new):
+        return new if old is None else jnp.maximum(old, new)
+
+    for row_set, lane_set in products:
+        cosine = lax.dot_general(
+            jnp.concatenate([row_refs[i][:rows, :] for i in row_set], axis=0),
+            jnp.concatenate([lane_refs[j][:rows, :] for j in lane_set], axis=0),
+            (((1,), (1,)), ((), ())),
+            preferred_element_type=jnp.float32,
+        )
+        for m, i in enumerate(row_set):
+            row_cluster, row_prio = columns[:, 2 * i:2 * i + 1], columns[:, 2 * i + 1:2 * i + 2]
+            for n, j in enumerate(lane_set):
+                lane_cluster, lane_prio = lane_notes[j]
+                here = cosine[m * rows:(m + 1) * rows, n * rows:(n + 1) * rows]
+                same = jnp.where(row_cluster == lane_cluster, here, -1.0)
+                earlier = row_prio < lane_prio
+                best[j] = top(best[j], jnp.where(earlier, same, -1.0))
+                if j > 0:
+                    back[i] = top(back[i], jnp.where(earlier, -1.0, same))
+    lane_ids = lax.broadcasted_iota(jnp.int32, (rows, rows), 1)
     table = jnp.full((rows, rows), -1.0, jnp.float32)
-    lane_ids = lax.broadcasted_iota(jnp.int32, (rows, rows), 1)
-    for i in range(row_count):
-        row_cluster, row_prio = columns[:, 2 * i:2 * i + 1], columns[:, 2 * i + 1:2 * i + 2]
-        back = jnp.full((rows, rows), -1.0, jnp.float32)
-        for j, (lane_cluster, lane_prio) in enumerate(lane_notes):
-            here = cosine[i * rows:(i + 1) * rows, j * rows:(j + 1) * rows]
-            same = jnp.where(row_cluster == lane_cluster, here, -1.0)
-            earlier = row_prio < lane_prio
-            best[j] = jnp.maximum(best[j], jnp.where(earlier, same, -1.0))
-            if j > 0:
-                back = jnp.maximum(back, jnp.where(earlier, -1.0, same))
-        table = jnp.where(lane_ids == i, jnp.max(back, axis=1, keepdims=True), table)
+    for i in back_rows:
+        table = jnp.where(lane_ids == i, jnp.max(back[i], axis=1, keepdims=True), table)
     table = table.T
-    for i, ref in enumerate(back_outs):
+    for i in back_rows:
         line = table[i:i + 1]
-        ref[...] = jnp.maximum(line, seen_backs[i][...]) if has_backs else line
+        refs.pop(0)[...] = jnp.maximum(line, seen_backs[i][...]) if i in seen_backs else line
     lines = jnp.concatenate([jnp.max(b, axis=0, keepdims=True) for b in best], axis=0)
-    lines_out[...] = jnp.maximum(lines, seen_lines[...]) if has_lines else lines
-
-
-def score(name, row_blocks, lane_blocks, lines=(), backs=(), hold=False):
+    if has_lines:
+        count = seen_lines.shape[0]
+        first = jnp.maximum(lines[:count], seen_lines[...])
+        lines = first if count == lane_count else jnp.concatenate([first, lines[count:]], axis=0)
+    lines_out[...] = lines
+
+
+def score(name, row_blocks, lane_blocks, products, back_rows, lines=None, backs=None, hold=False):
     high, width = row_blocks[0].shape
     rows = high - NOTE_ROWS
-    inputs = [*row_blocks, *lane_blocks, *lines, *backs]
-    shapes = [(len(lane_blocks), rows)] + [(1, rows)] * len(row_blocks)
+    backs = backs or {}
+    inputs = [*row_blocks, *lane_blocks, *([] if lines is None else [lines]), *backs.values()]
+    shapes = [(len(lane_blocks), rows)] + [(1, rows)] * len(back_rows)
     outs = [jax.ShapeDtypeStruct(shape, jnp.float32) for shape in shapes]
     if hold:
         outs.append(jax.ShapeDtypeStruct((high, width), row_blocks[0].dtype))
     counts = len(row_blocks), len(lane_blocks)
-    flags = len(lines) > 0, len(backs) > 0, hold
+    rest = products, back_rows, lines is not None, tuple(backs), hold
+    macs = sum(len(r) * len(c) for r, c in products) * rows * rows * width
     return pl.pallas_call(
-        lambda *refs: score_kernel(*counts, *flags, *refs),
+        lambda *refs: score_kernel(*counts, *rest, *refs),
         in_specs=[VMEM] * len(inputs),
         out_specs=[VMEM] * len(outs),
         out_shape=outs,
         compiler_params=pltpu.CompilerParams(vmem_limit_bytes=48 << 20),
         cost_estimate=pl.CostEstimate(
-            flops=2 * math.prod(counts) * rows * rows * width,
-            bytes_accessed=2 * sum(counts) * rows * width,
-            transcendentals=0,
+            flops=2 * macs, bytes_accessed=2 * sum(counts) * rows * width, transcendentals=0
         ),
         name=name,
     )(*inputs)
 
 
 def tournament(line):
-    moves = [[(i, (i + s) % line) for i in range(line)] for s in range(1, (line + 1) // 2)]
+    moves = [[(i, (i - s) % line) for i in range(line)] for s in range(1, (line + 1) // 2)]
     if line % 2 == 0:
         half = line // 2
         pairs = [(i, i + half) if i % 2 else (i + half, i) for i in range(half)]
@@ -191,20 +201,34 @@
     steps = range(2, plane, 2)
     plane_blocks = [swap(block, step) for step in steps]
 
-    soon, last = plane_blocks[:-2], plane_blocks[-2:]
-    lines, *backs, held = score("score_soon", [block] + soon, [block] + visitors, hold=True)
-    lanes = [held] + visitors
-    lines, *more = score("score_late", last, lanes, lines=[lines])
-    lanes = [swap(block, 1)] + [swap(visitor, 1) for visitor in visitors]
-    theirs, own_back, *backs = score(
-        "score_partner", [held] + soon + last, lanes, backs=backs + more
-    )
+    lanes = [block] + visitors
+    every, count = tuple(range(len(lanes))), 1 + len(plane_blocks)
+    most = tuple(range(count - 1))
+    lines, *backs, held = score(
+        "score_soon", [block] + plane_blocks[:-1], lanes[:-1], [(most, every[:-1])], most, hold=True
+    )
+    row_blocks = [held] + plane_blocks
+    lanes[0] = lax.optimization_barrier((block, visitors[0]))[0]
+    lanes[-1] = lax.optimization_barrier((lanes[-1], held))[0]
+    partner = [swap(lane, 1) for lane in lanes]
+    products = [(most + (count - 1,), every)]
+    theirs, *backs = score(
+        "score_partner", row_blocks, partner, products, most + (count - 1,), backs=dict(enumerate(backs))
+    )
+    lanes[0] = held
+    products = [((count - 1,), every), (most, every[-1:])]
+    lines, *backs = score(
+        "score_late", row_blocks, lanes, products, most + (count - 1,), lines, dict(enumerate(backs))
+    )
+    own_back, *backs = backs
     lines = jnp.maximum(lines, swap(theirs, 1))
     total = jnp.maximum(lines[:1], own_back)
-    for step, back in zip(steps, backs):
-        total = jnp.maximum(total, swap(back, step))
     for i, pairs in enumerate(moves):
         total = jnp.maximum(total, move(lines[i + 1:i + 2], [(b, a) for a, b in pairs]))
+    for i, (step, back) in enumerate(zip(steps, backs)):
+        if i == 1:
+            total = lax.optimization_barrier(total)
+        total = jnp.maximum(total, swap(back, step))
     return total.reshape(rows)
 
 

time: 31.9 us -> 33.7 us (1.056)
  waiting for transfers between devices: 10 us -> 11.3 us
  starting transfers between devices: 15.1 us -> 15.6 us
    ppermute x10, waiting for transfers between devices: 0.2 us -> 8.13 us  [swap(): return lax.ppermute(array, AXES, pairs)]
    ppermute x4, waiting for transfers between devices: 9.83 us -> 3.17 us  [move(): return lax.ppermute(array, AXES, whole)]
  transfers between devices with their start and end apart: 14 -> 14, of which waited for: 5 -> 9; matrix products, arithmetic and copies ran while one was open for 0% -> 0% of each run, Pallas kernels for 3% -> 3%
where the time goes in v1:
time: 33.7 us; the launch traced here: 33.6 us
  starting transfers between devices  15.6 us (46%)
  waiting for transfers between devices  11.3 us (34%)
  Pallas kernels  5.22 us (15%)
  local copies, waits for them, and re-layouts  0.94 us (3%)
  other arithmetic  0.52 us (2%)
    ppermute x10, waiting for transfers between devices, swap(): return lax.ppermute(array, AXES, pairs)  8.13 us
    ppermute x10, starting transfers between devices, swap(): return lax.ppermute(array, AXES, pairs)  7.81 us
    ppermute x4, starting transfers between devices, move(): return lax.ppermute(array, AXES, whole)  7.74 us
    pallas_call x1, Pallas kernels, embed(): pl.pallas_call(embed_kernel, in_specs=[HBM] * 5, out_specs=VMEM, out_shap...  3.31 us
    ppermute x4, waiting for transfers between devices, move(): return lax.ppermute(array, AXES, whole)  3.17 us
    pallas_call x3, Pallas kernels, score(): pl.pallas_call(lambda *refs: score_kernel(*counts, *rest, *refs), in_spec...  1.91 us
    unnamed x2, local copies, waits for them, and re-layouts  0.93 us
  transfers between devices with their start and end apart: 14, of which 9 were waited for; matrix products, arithmetic and copies ran while one was open for 0% of the time, Pallas kernels for 3%

profile of v1, /device:TPU:0, one launch (start us, length us, event | category | flops | bytes accessed | tf_op | source)
XLA Modules:
  0.0 33.6 jit_solution(15558653504189089738)
XLA Ops:
  0.0 3.3 %embed.1.refs_0_.refs_3_ = bf16[136,768]{1,0:T(8,128)(2,1)} custom-call(bf16[128,2048]{1,0:T(8,128)(2,1)} %states_hbm.1, bf16[2048,768]{1,0:T(8,128)(2,1)} %proj_hbm.1, s32[1,128]{1,0:T(1,128)} %bitcast.5, s32[1,128]{1,0:T(1,128)} %bitcast.6, s32[1,128]{1,0:T(1,128)} %bitcast.7), custom_call_target="tpu_custom_call" | custom-call | tf_op jit(solution)/shard_map/embed/pallas_call | solution.py:64
  3.3 5.1 %collective-permute-start.2 = (bf16[136,768]{1,0:T(8,128)(2,1)}, bf16[136,768]{1,0:T(8,128)(2,1)S(1)}, u32[]{:S(2)}, u32[]{:S(2)}) collective-permute-start(bf16[136,768]{1,0:T(8,128)(2,1)} %embed.1.refs_0_.refs_3_), channel_id=1, source_target_pairs={{0,24},{1,25},{2,26},{3,27},{4,28},{5,29},{6,30},{7,31},{8,0},{9,1... | collective-permute-start | bytes 626696 | tf_op jit(solution)/shard_map/ppermute | solution.py:186
  8.4 1.5 %collective-permute-start.1 = (bf16[136,768]{1,0:T(8,128)(2,1)}, bf16[136,768]{1,0:T(8,128)(2,1)S(1)}, u32[]{:S(2)}, u32[]{:S(2)}) collective-permute-start(bf16[136,768]{1,0:T(8,128)(2,1)} %embed.1.refs_0_.refs_3_), channel_id=1, source_target_pairs={{0,4},{1,5},{2,6},{3,7},{4,0},{5,1},{6,2},{7,3},{8,12},{9,13},{10,... | collective-permute-start | bytes 626696 | tf_op jit(solution)/shard_map/ppermute | solution.py:190
  9.9 1.5 %collective-permute-start = (bf16[136,768]{1,0:T(8,128)(2,1)}, bf16[136,768]{1,0:T(8,128)(2,1)S(1)}, u32[]{:S(2)}, u32[]{:S(2)}) collective-permute-start(bf16[136,768]{1,0:T(8,128)(2,1)} %embed.1.refs_0_.refs_3_), channel_id=1, source_target_pairs={{0,2},{1,3},{2,0},{3,1},{4,6},{5,7},{6,4},{7,5},{8,10},{9,11},{10,... | collective-permute-start | bytes 626696 | tf_op jit(solution)/shard_map/ppermute | solution.py:190
  11.4 0.5 %collective-permute-start.3 = (bf16[136,768]{1,0:T(8,128)(2,1)}, bf16[136,768]{1,0:T(8,128)(2,1)S(1)}, u32[]{:S(2)}, u32[]{:S(2)}) collective-permute-start(bf16[136,768]{1,0:T(8,128)(2,1)} %embed.1.refs_0_.refs_3_), channel_id=1, source_target_pairs={{0,6},{1,7},{2,4},{3,5},{4,2},{5,3},{6,0},{7,1},{8,14},{9,15},{10,... | collective-permute-start | bytes 626696 | tf_op jit(solution)/shard_map/ppermute | solution.py:190
  11.9 2.4 %collective-permute-done.2.refs_4_.refs_5_ = bf16[136,768]{1,0:T(8,128)(2,1)S(1)} collective-permute-done((bf16[136,768]{1,0:T(8,128)(2,1)}, bf16[136,768]{1,0:T(8,128)(2,1)S(1)}, u32[]{:S(2)}, u32[]{:S(2)}) %collective-permute-start.2) | collective-permute-done | bytes 208928 | tf_op jit(solution)/shard_map/ppermute | solution.py:186
  14.3 1.5 %collective-permute-done.1.refs_2_ = bf16[136,768]{1,0:T(8,128)(2,1)S(1)} collective-permute-done((bf16[136,768]{1,0:T(8,128)(2,1)}, bf16[136,768]{1,0:T(8,128)(2,1)S(1)}, u32[]{:S(2)}, u32[]{:S(2)}) %collective-permute-start.1) | collective-permute-done | bytes 208928 | tf_op jit(solution)/shard_map/ppermute | solution.py:190
  15.8 2.4 %collective-permute-done.refs_1_ = bf16[136,768]{1,0:T(8,128)(2,1)S(1)} collective-permute-done((bf16[136,768]{1,0:T(8,128)(2,1)}, bf16[136,768]{1,0:T(8,128)(2,1)S(1)}, u32[]{:S(2)}, u32[]{:S(2)}) %collective-permute-start) | collective-permute-done | bytes 208928 | tf_op jit(solution)/shard_map/ppermute | solution.py:190
  18.3 0.9 %copy-done = bf16[136,768]{1,0:T(8,128)(2,1)S(1)} copy-done((bf16[136,768]{1,0:T(8,128)(2,1)S(1)}, bf16[136,768]{1,0:T(8,128)(2,1)}, u32[]{:S(2)}) %copy-start) | copy-done | bytes 208920
  19.2 0.6 %score_soon.1 = (f32[2,128]{1,0:T(2,128)S(1)}, f32[1,128]{1,0:T(1,128)S(1)}, f32[1,128]{1,0:T(1,128)S(1)}, f32[1,128]{1,0:T(1,128)S(1)}, bf16[136,768]{1,0:T(8,128)(2,1)S(1)}) custom-call(bf16[136,768]{1,0:T(8,128)(2,1)S(1)} %copy-done, bf16[136,768]{1,0:T(8,128)(2,1)S(1)} %collective-permute-done.refs_1_, ...), custom_call_target="tpu_custom_call" | custom-call | flops 150994944 | bytes 983040 | tf_op jit(solution)/shard_map/score_soon/pallas_call | solution.py:154
  19.8 0.5 %collective-permute-start.7 = (bf16[136,768]{1,0:T(8,128)(2,1)S(1)}, bf16[136,768]{1,0:T(8,128)(2,1)S(1)}, u32[]{:S(2)}, u32[]{:S(2)}) collective-permute-start(bf16[136,768]{1,0:T(8,128)(2,1)S(1)} %collective-permute-done.4.refs_6_), channel_id=1, source_target_pairs={{0,1},{1,0},{2,3},{3,2},{4,5},{5,4},{6,7},{7,6},{8,9},{9,8},{10,11... | collective-permute-start | bytes 626696 | tf_op jit(solution)/shard_map/ppermute | solution.py:190
  20.3 0.6 %collective-permute-done.3.refs_3_ = bf16[136,768]{1,0:T(8,128)(2,1)S(1)} collective-permute-done((bf16[136,768]{1,0:T(8,128)(2,1)}, bf16[136,768]{1,0:T(8,128)(2,1)S(1)}, u32[]{:S(2)}, u32[]{:S(2)}) %collective-permute-start.3) | collective-permute-done | bytes 208928 | tf_op jit(solution)/shard_map/ppermute | solution.py:190
  20.9 0.3 collective-permute-done.6.refs_5_
  21.5 0.7 %score_partner.1 = (f32[3,128]{1,0:T(4,128)S(1)}, f32[1,128]{1,0:T(1,128)S(1)}, f32[1,128]{1,0:T(1,128)S(1)}, f32[1,128]{1,0:T(1,128)S(1)}, f32[1,128]{1,0:T(1,128)S(1)}) custom-call(bf16[136,768]{1,0:T(8,128)(2,1)S(1)} %get-tuple-element.22.refs_0_.refs_4_, bf16[136,768]{1,0:T(8,128)(2,1)S(1)} %collective-permute-done.refs_1_, ...), custom_call_target="tpu_custom_call" | custom-call | flops 301989888 | bytes 1376256 | tf_op jit(solution)/shard_map/score_partner/pallas_call | solution.py:154
  22.5 0.6 %score_late.1 = (f32[3,128]{1,0:T(4,128)S(1)}, f32[1,128]{1,0:T(1,128)S(1)}, f32[1,128]{1,0:T(1,128)S(1)}, f32[1,128]{1,0:T(1,128)S(1)}, f32[1,128]{1,0:T(1,128)S(1)}) custom-call(bf16[136,768]{1,0:T(8,128)(2,1)S(1)} %get-tuple-element.22.refs_0_.refs_4_, bf16[136,768]{1,0:T(8,128)(2,1)S(1)} %collective-permute-done.refs_1_, ...), custom_call_target="tpu_custom_call" | custom-call | flops 150994944 | bytes 1376256 | tf_op jit(solution)/shard_map/score_late/pallas_call | solution.py:154
  23.2 1.5 %collective-permute-start.11 = (f32[1,128]{1,0:T(1,128)S(1)}, f32[1,128]{1,0:T(1,128)S(1)}, u32[]{:S(2)}, u32[]{:S(2)}) collective-permute-start(f32[1,128]{1,0:T(1,128)S(1)} %get-tuple-element.36), channel_id=1, source_target_pairs={{0,2},{1,3},{2,0},{3,1},{4,6},{5,7},{6,4},{7,5},{8,10},{9,11},{10,... | collective-permute-start | bytes 1544 | tf_op jit(solution)/shard_map/ppermute | solution.py:190
  24.7 0.3 collective-permute-start.9
  25.0 2.3 %collective-permute-start.10 = (f32[1,128]{1,0:T(1,128)S(1)}, f32[1,128]{1,0:T(1,128)S(1)}, u32[]{:S(2)}, u32[]{:S(2)}) collective-permute-start(f32[1,128]{1,0:T(1,128)S(1)} %get-tuple-element.40), channel_id=1, source_target_pairs={{0,16},{1,17},{2,18},{3,19},{4,20},{5,21},{6,22},{7,23},{24,8},{25... | collective-permute-start | bytes 1544 | tf_op jit(solution)/shard_map/ppermute | solution.py:186
  27.3 1.3 %collective-permute-start.12 = (f32[1,128]{1,0:T(1,128)S(1)}, f32[1,128]{1,0:T(1,128)S(1)}, u32[]{:S(2)}, u32[]{:S(2)}) collective-permute-start(f32[1,128]{1,0:T(1,128)S(1)} %get-tuple-element.37), channel_id=1, source_target_pairs={{0,4},{1,5},{2,6},{3,7},{4,0},{5,1},{6,2},{7,3},{8,12},{9,13},{10,... | collective-permute-start | bytes 1544 | tf_op jit(solution)/shard_map/ppermute | solution.py:190
  28.6 0.7 %collective-permute-start.13 = (f32[1,128]{1,0:T(1,128)S(1)}, f32[1,128]{1,0:T(1,128)S(1)}, u32[]{:S(2)}, u32[]{:S(2)}) collective-permute-start(f32[1,128]{1,0:T(1,128)S(1)} %get-tuple-element.38), channel_id=1, source_target_pairs={{0,6},{1,7},{2,4},{3,5},{4,2},{5,3},{6,0},{7,1},{8,14},{9,15},{10,... | collective-permute-start | bytes 1544 | tf_op jit(solution)/shard_map/ppermute | solution.py:190
  29.3 0.8 %collective-permute-done.9 = f32[1,128]{1,0:T(1,128)S(1)} collective-permute-done((f32[1,128]{1,0:T(1,128)S(1)}, f32[1,128]{1,0:T(1,128)S(1)}, u32[]{:S(2)}, u32[]{:S(2)}) %collective-permute-start.9) | collective-permute-done | bytes 544 | tf_op jit(solution)/shard_map/ppermute | solution.py:186
  30.1 0.8 %collective-permute-done.12 = f32[1,128]{1,0:T(1,128)S(1)} collective-permute-done((f32[1,128]{1,0:T(1,128)S(1)}, f32[1,128]{1,0:T(1,128)S(1)}, u32[]{:S(2)}, u32[]{:S(2)}) %collective-permute-start.12) | collective-permute-done | bytes 544 | tf_op jit(solution)/shard_map/ppermute | solution.py:190
  30.9 2.2 %collective-permute-done.13 = f32[1,128]{1,0:T(1,128)S(1)} collective-permute-done((f32[1,128]{1,0:T(1,128)S(1)}, f32[1,128]{1,0:T(1,128)S(1)}, u32[]{:S(2)}, u32[]{:S(2)}) %collective-permute-start.13) | collective-permute-done | bytes 544 | tf_op jit(solution)/shard_map/ppermute | solution.py:190
  33.1 0.5 %maximum_bitcast_fusion = f32[128]{0:T(128)} fusion(f32[1,128]{1,0:T(1,128)S(1)} %collective-permute-done.13, f32[1,128]{1,0:T(1,128)S(1)} %maximum_maximum_fusion, f32[1,128]{1,0:T(1,128)S(1)} %collective-permute-done.12), kind=kLoop, calls=%fused_computation | loop fusion | flops 256 | bytes 2048 | tf_op jit(solution)/shard_map/reshape | solution.py:232
  (14 shorter events, 0.6 us)
Async XLA Ops:
  3.3 11.0 %collective-permute-start.2 = (bf16[136,768]{1,0:T(8,128)(2,1)}, bf16[136,768]{1,0:T(8,128)(2,1)S(1)}, u32[]{:S(2)}, u32[]{:S(2)}) collective-permute-start(bf16[136,768]{1,0:T(8,128)(2,1)} %embed.1.refs_0_.refs_3_), channel_id=1, source_target_pairs={{0,24},{1,25},{2,26},{3,27},{4,28},{5,29},{6,30},{7,31},{8,0},{9,1... | collective-permute-start | bytes 626696 | tf_op jit(solution)/shard_map/ppermute | solution.py:186
  8.4 7.4 %collective-permute-start.1 = (bf16[136,768]{1,0:T(8,128)(2,1)}, bf16[136,768]{1,0:T(8,128)(2,1)S(1)}, u32[]{:S(2)}, u32[]{:S(2)}) collective-permute-start(bf16[136,768]{1,0:T(8,128)(2,1)} %embed.1.refs_0_.refs_3_), channel_id=1, source_target_pairs={{0,4},{1,5},{2,6},{3,7},{4,0},{5,1},{6,2},{7,3},{8,12},{9,13},{10,... | collective-permute-start | bytes 626696 | tf_op jit(solution)/shard_map/ppermute | solution.py:190
  9.9 8.3 %collective-permute-start = (bf16[136,768]{1,0:T(8,128)(2,1)}, bf16[136,768]{1,0:T(8,128)(2,1)S(1)}, u32[]{:S(2)}, u32[]{:S(2)}) collective-permute-start(bf16[136,768]{1,0:T(8,128)(2,1)} %embed.1.refs_0_.refs_3_), channel_id=1, source_target_pairs={{0,2},{1,3},{2,0},{3,1},{4,6},{5,7},{6,4},{7,5},{8,10},{9,11},{10,... | collective-permute-start | bytes 626696 | tf_op jit(solution)/shard_map/ppermute | solution.py:190
  11.4 8.3 %collective-permute-start.4 = (bf16[136,768]{1,0:T(8,128)(2,1)}, bf16[136,768]{1,0:T(8,128)(2,1)S(1)}, u32[]{:S(2)}, u32[]{:S(2)}) collective-permute-start(bf16[136,768]{1,0:T(8,128)(2,1)} %embed.1.refs_0_.refs_3_), channel_id=1, source_target_pairs={{16,0},{17,1},{18,2},{19,3},{20,4},{21,5},{22,6},{23,7},{8,24},{9,... | collective-permute-start | bytes 626696 | tf_op jit(solution)/shard_map/ppermute | solution.py:186
  11.4 9.5 %collective-permute-start.3 = (bf16[136,768]{1,0:T(8,128)(2,1)}, bf16[136,768]{1,0:T(8,128)(2,1)S(1)}, u32[]{:S(2)}, u32[]{:S(2)}) collective-permute-start(bf16[136,768]{1,0:T(8,128)(2,1)} %embed.1.refs_0_.refs_3_), channel_id=1, source_target_pairs={{0,6},{1,7},{2,4},{3,5},{4,2},{5,3},{6,0},{7,1},{8,14},{9,15},{10,... | collective-permute-start | bytes 626696 | tf_op jit(solution)/shard_map/ppermute | solution.py:190
  14.3 6.6 %collective-permute-start.5 = (bf16[136,768]{1,0:T(8,128)(2,1)}, bf16[136,768]{1,0:T(8,128)(2,1)S(1)}, u32[]{:S(2)}, u32[]{:S(2)}) collective-permute-start(bf16[136,768]{1,0:T(8,128)(2,1)} %embed.1.refs_0_.refs_3_), channel_id=1, source_target_pairs={{0,1},{1,0},{2,3},{3,2},{4,5},{5,4},{6,7},{7,6},{8,9},{9,8},{10,11... | collective-permute-start | bytes 626696 | tf_op jit(solution)/shard_map/ppermute | solution.py:190
  18.3 0.9 %copy-start = (bf16[136,768]{1,0:T(8,128)(2,1)S(1)}, bf16[136,768]{1,0:T(8,128)(2,1)}, u32[]{:S(2)}) copy-start(bf16[136,768]{1,0:T(8,128)(2,1)} %embed.1.refs_0_.refs_3_) | copy-start | bytes 626692
  19.7 1.5 %collective-permute-start.6 = (bf16[136,768]{1,0:T(8,128)(2,1)S(1)}, bf16[136,768]{1,0:T(8,128)(2,1)S(1)}, u32[]{:S(2)}, u32[]{:S(2)}) collective-permute-start(bf16[136,768]{1,0:T(8,128)(2,1)S(1)} %collective-permute-done.2.refs_4_.refs_5_), channel_id=1, source_target_pairs={{0,1},{1,0},{2,3},{3,2},{4,5},{5,4},{6,7},{7,6},{8,9},{9,8},{10,11... | collective-permute-start | bytes 626696 | tf_op jit(solution)/shard_map/ppermute | solution.py:190
  19.8 1.7 %collective-permute-start.7 = (bf16[136,768]{1,0:T(8,128)(2,1)S(1)}, bf16[136,768]{1,0:T(8,128)(2,1)S(1)}, u32[]{:S(2)}, u32[]{:S(2)}) collective-permute-start(bf16[136,768]{1,0:T(8,128)(2,1)S(1)} %collective-permute-done.4.refs_6_), channel_id=1, source_target_pairs={{0,1},{1,0},{2,3},{3,2},{4,5},{5,4},{6,7},{7,6},{8,9},{9,8},{10,11... | collective-permute-start | bytes 626696 | tf_op jit(solution)/shard_map/ppermute | solution.py:190
  22.3 2.4 %collective-permute-start.8 = (f32[3,128]{1,0:T(4,128)S(1)}, f32[3,128]{1,0:T(4,128)S(1)}, u32[]{:S(2)}, u32[]{:S(2)}) collective-permute-start(f32[3,128]{1,0:T(4,128)S(1)} %get-tuple-element.34), channel_id=1, source_target_pairs={{0,1},{1,0},{2,3},{3,2},{4,5},{5,4},{6,7},{7,6},{8,9},{9,8},{10,11... | collective-permute-start | bytes 4616 | tf_op jit(solution)/shard_map/ppermute | solution.py:190
  23.2 6.2 %collective-permute-start.11 = (f32[1,128]{1,0:T(1,128)S(1)}, f32[1,128]{1,0:T(1,128)S(1)}, u32[]{:S(2)}, u32[]{:S(2)}) collective-permute-start(f32[1,128]{1,0:T(1,128)S(1)} %get-tuple-element.36), channel_id=1, source_target_pairs={{0,2},{1,3},{2,0},{3,1},{4,6},{5,7},{6,4},{7,5},{8,10},{9,11},{10,... | collective-permute-start | bytes 1544 | tf_op jit(solution)/shard_map/ppermute | solution.py:190
  24.7 5.4 %collective-permute-start.9 = (f32[1,128]{1,0:T(1,128)S(1)}, f32[1,128]{1,0:T(1,128)S(1)}, u32[]{:S(2)}, u32[]{:S(2)}) collective-permute-start(f32[1,128]{1,0:T(1,128)S(1)} %get-tuple-element.39), channel_id=1, source_target_pairs={{24,0},{25,1},{26,2},{27,3},{28,4},{29,5},{30,6},{31,7},{0,8},{1,9... | collective-permute-start | bytes 1544 | tf_op jit(solution)/shard_map/ppermute | solution.py:186
  25.0 5.1 %collective-permute-start.10 = (f32[1,128]{1,0:T(1,128)S(1)}, f32[1,128]{1,0:T(1,128)S(1)}, u32[]{:S(2)}, u32[]{:S(2)}) collective-permute-start(f32[1,128]{1,0:T(1,128)S(1)} %get-tuple-element.40), channel_id=1, source_target_pairs={{0,16},{1,17},{2,18},{3,19},{4,20},{5,21},{6,22},{7,23},{24,8},{25... | collective-permute-start | bytes 1544 | tf_op jit(solution)/shard_map/ppermute | solution.py:186
  27.3 3.5 %collective-permute-start.12 = (f32[1,128]{1,0:T(1,128)S(1)}, f32[1,128]{1,0:T(1,128)S(1)}, u32[]{:S(2)}, u32[]{:S(2)}) collective-permute-start(f32[1,128]{1,0:T(1,128)S(1)} %get-tuple-element.37), channel_id=1, source_target_pairs={{0,4},{1,5},{2,6},{3,7},{4,0},{5,1},{6,2},{7,3},{8,12},{9,13},{10,... | collective-permute-start | bytes 1544 | tf_op jit(solution)/shard_map/ppermute | solution.py:190
  28.6 4.4 %collective-permute-start.13 = (f32[1,128]{1,0:T(1,128)S(1)}, f32[1,128]{1,0:T(1,128)S(1)}, u32[]{:S(2)}, u32[]{:S(2)}) collective-permute-start(f32[1,128]{1,0:T(1,128)S(1)} %get-tuple-element.38), channel_id=1, source_target_pairs={{0,6},{1,7},{2,4},{3,5},{4,2},{5,3},{6,0},{7,1},{8,14},{9,15},{10,... | collective-permute-start | bytes 1544 | tf_op jit(solution)/shard_map/ppermute | solution.py:190

commit v2 on v1

--- a/solution.py
+++ b/solution.py
@@ -86,12 +86,12 @@
     return (owner - 1.0) * 4.0 + sub, high * float(RADIX) + low
 
 
-def score_kernel(row_count, lane_count, products, back_rows, has_lines, seen_rows, hold, *refs):
+def score_kernel(row_count, lane_count, products, parts, has_lines, seen_rows, hold, *refs):
     refs = list(refs)
     row_refs = [refs.pop(0) for _ in range(row_count)]
     lane_refs = [refs.pop(0) for _ in range(lane_count)]
     seen_lines = refs.pop(0) if has_lines else None
-    seen_backs = {i: refs.pop(0) for i in seen_rows}
+    seen_backs = refs.pop(0) if seen_rows else None
     lines_out = refs.pop(0)
     rows = lines_out.shape[1]
     if hold:
@@ -125,12 +125,14 @@
                     back[i] = top(back[i], jnp.where(earlier, -1.0, same))
     lane_ids = lax.broadcasted_iota(jnp.int32, (rows, rows), 1)
     table = jnp.full((rows, rows), -1.0, jnp.float32)
-    for i in back_rows:
-        table = jnp.where(lane_ids == i, jnp.max(back[i], axis=1, keepdims=True), table)
+    for i, each in enumerate(back):
+        if each is not None:
+            table = jnp.where(lane_ids == i, jnp.max(each, axis=1, keepdims=True), table)
     table = table.T
-    for i in back_rows:
-        line = table[i:i + 1]
-        refs.pop(0)[...] = jnp.maximum(line, seen_backs[i][...]) if i in seen_backs else line
+    if seen_rows:
+        table = jnp.maximum(table[:row_count], seen_backs[...])
+    for first, stop in parts:
+        refs.pop(0)[...] = table[first:stop]
     lines = jnp.concatenate([jnp.max(b, axis=0, keepdims=True) for b in best], axis=0)
     if has_lines:
         count = seen_lines.shape[0]
@@ -139,17 +141,16 @@
     lines_out[...] = lines
 
 
-def score(name, row_blocks, lane_blocks, products, back_rows, lines=None, backs=None, hold=False):
+def score(name, row_blocks, lane_blocks, products, parts, lines=None, backs=None, hold=False):
     high, width = row_blocks[0].shape
     rows = high - NOTE_ROWS
-    backs = backs or {}
-    inputs = [*row_blocks, *lane_blocks, *([] if lines is None else [lines]), *backs.values()]
-    shapes = [(len(lane_blocks), rows)] + [(1, rows)] * len(back_rows)
+    inputs = [*row_blocks, *lane_blocks, *(seen for seen in (lines, backs) if seen is not None)]
+    shapes = [(len(lane_blocks), rows)] + [(stop - first, rows) for first, stop in parts]
     outs = [jax.ShapeDtypeStruct(shape, jnp.float32) for shape in shapes]
     if hold:
         outs.append(jax.ShapeDtypeStruct((high, width), row_blocks[0].dtype))
     counts = len(row_blocks), len(lane_blocks)
-    rest = products, back_rows, lines is not None, tuple(backs), hold
+    rest = products, parts, lines is not None, backs is not None, hold
     macs = sum(len(r) * len(c) for r, c in products) * rows * rows * width
     return pl.pallas_call(
         lambda *refs: score_kernel(*counts, *rest, *refs),
@@ -165,7 +166,7 @@
 
 
 def tournament(line):
-    moves = [[(i, (i - s) % line) for i in range(line)] for s in range(1, (line + 1) // 2)]
+    moves = [[(i, (i + s) % line) for i in range(line)] for s in range(1, (line + 1) // 2)]
     if line % 2 == 0:
         half = line // 2
         pairs = [(i, i + half) if i % 2 else (i + half, i) for i in range(half)]
@@ -198,37 +199,38 @@
     )
     moves = tournament(line)
     visitors = [move(block, pairs) for pairs in moves]
-    steps = range(2, plane, 2)
-    plane_blocks = [swap(block, step) for step in steps]
+    bits = [1 << i for i in range(1, plane.bit_length() - 1)]
+    row_blocks = [block]
+    for bit in bits:
+        row_blocks += [swap(here, bit) for here in row_blocks]
 
     lanes = [block] + visitors
-    every, count = tuple(range(len(lanes))), 1 + len(plane_blocks)
-    most = tuple(range(count - 1))
-    lines, *backs, held = score(
-        "score_soon", [block] + plane_blocks[:-1], lanes[:-1], [(most, every[:-1])], most, hold=True
-    )
-    row_blocks = [held] + plane_blocks
-    lanes[0] = lax.optimization_barrier((block, visitors[0]))[0]
-    lanes[-1] = lax.optimization_barrier((lanes[-1], held))[0]
-    partner = [swap(lane, 1) for lane in lanes]
-    products = [(most + (count - 1,), every)]
-    theirs, *backs = score(
-        "score_partner", row_blocks, partner, products, most + (count - 1,), backs=dict(enumerate(backs))
-    )
+    every, count = tuple(range(len(lanes))), len(row_blocks)
+    most, last = tuple(range(count - 1)), (count - 1,)
+    lines, backs, held = score(
+        "score_soon", row_blocks[:-1], lanes[:-1], [(most, every[:-1])], [(0, count)], hold=True
+    )
+    row_blocks[0] = held
+    order = lax.optimization_barrier((lanes[0], row_blocks[-2]))[0]
+    partner = [swap(lane, 1) for lane in [order] + visitors]
     lanes[0] = held
-    products = [((count - 1,), every), (most, every[-1:])]
-    lines, *backs = score(
-        "score_late", row_blocks, lanes, products, most + (count - 1,), lines, dict(enumerate(backs))
-    )
-    own_back, *backs = backs
+    products = [(last, every), (most, every[-1:])]
+    lines, backs = score(
+        "score_late", row_blocks, lanes, products, [(0, count)], lines, backs
+    )
+    half = count // 2
+    products, parts = [(most + last, every)], [(0, half), (half, count)]
+    theirs, near, far = score("score_partner", row_blocks, partner, products, parts, None, backs)
     lines = jnp.maximum(lines, swap(theirs, 1))
-    total = jnp.maximum(lines[:1], own_back)
-    for i, pairs in enumerate(moves):
+    for bit in bits[:0:-1]:
+        near = jnp.maximum(near, swap(far, bit))
+        half = near.shape[0] // 2
+        near, far = near[:half], near[half:]
+    total = lines[:1]
+    for i, pairs in reversed(list(enumerate(moves))):
         total = jnp.maximum(total, move(lines[i + 1:i + 2], [(b, a) for a, b in pairs]))
-    for i, (step, back) in enumerate(zip(steps, backs)):
-        if i == 1:
-            total = lax.optimization_barrier(total)
-        total = jnp.maximum(total, swap(back, step))
+    total = lax.optimization_barrier(total)
+    total = jnp.maximum(jnp.maximum(total, near), swap(far, bits[0]))
     return total.reshape(rows)
 
 

time: 33.7 us -> 32 us (0.950)
  starting transfers between devices: 15.6 us -> 13.1 us
  waiting for transfers between devices: 11.3 us -> 12 us
    ppermute x4, waiting for transfers between devices: 3.17 us -> 9.6 us  [move(): return lax.ppermute(array, AXES, whole)]
    ppermute x10 -> x9, waiting for transfers between devices: 8.13 us -> 2.4 us  [swap(): return lax.ppermute(array, AXES, pairs)]
    ppermute x4, starting transfers between devices: 7.74 us -> 5.21 us  [move(): return lax.ppermute(array, AXES, whole)]
    ppermute x10 -> x9, starting transfers between devices: 7.81 us -> 7.89 us  [swap(): return lax.ppermute(array, AXES, pairs)]
  transfers between devices with their start and end apart: 14 -> 13, of which waited for: 9 -> 8; matrix products, arithmetic and copies ran while one was open for 0% -> 0% of each run, Pallas kernels for 3% -> 4%
where the time goes in v2:
time: 32 us; the launch traced here: 31.8 us
  starting transfers between devices  13.1 us (41%)
  waiting for transfers between devices  12 us (38%)
  Pallas kernels  5.23 us (16%)
  local copies, waits for them, and re-layouts  0.94 us (3%)
  other arithmetic  0.52 us (2%)
    ppermute x4, waiting for transfers between devices, move(): return lax.ppermute(array, AXES, whole)  9.6 us
    ppermute x9, starting transfers between devices, swap(): return lax.ppermute(array, AXES, pairs)  7.89 us
    ppermute x4, starting transfers between devices, move(): return lax.ppermute(array, AXES, whole)  5.21 us
    pallas_call x1, Pallas kernels, embed(): pl.pallas_call(embed_kernel, in_specs=[HBM] * 5, out_specs=VMEM, out_shap...  3.31 us
    ppermute x9, waiting for transfers between devices, swap(): return lax.ppermute(array, AXES, pairs)  2.4 us
    pallas_call x3, Pallas kernels, score(): pl.pallas_call(lambda *refs: score_kernel(*counts, *rest, *refs), in_spec...  1.92 us
    unnamed x2, local copies, waits for them, and re-layouts  0.93 us
  transfers between devices with their start and end apart: 13, of which 8 were waited for; matrix products, arithmetic and copies ran while one was open for 0% of the time, Pallas kernels for 4%

profile of v2, /device:TPU:0, one launch (start us, length us, event | category | flops | bytes accessed | tf_op | source)
XLA Modules:
  0.0 31.8 jit_solution(14584005065137413675)
XLA Ops:
  0.0 3.3 %embed.1.refs_0_.refs_3_ = bf16[136,768]{1,0:T(8,128)(2,1)} custom-call(bf16[128,2048]{1,0:T(8,128)(2,1)} %states_hbm.1, bf16[2048,768]{1,0:T(8,128)(2,1)} %proj_hbm.1, s32[1,128]{1,0:T(1,128)} %bitcast.5, s32[1,128]{1,0:T(1,128)} %bitcast.6, s32[1,128]{1,0:T(1,128)} %bitcast.7), custom_call_target="tpu_custom_call" | custom-call | tf_op jit(solution)/shard_map/embed/pallas_call | solution.py:64
  3.3 3.0 %collective-permute-start = (bf16[136,768]{1,0:T(8,128)(2,1)}, bf16[136,768]{1,0:T(8,128)(2,1)S(1)}, u32[]{:S(2)}, u32[]{:S(2)}) collective-permute-start(bf16[136,768]{1,0:T(8,128)(2,1)} %embed.1.refs_0_.refs_3_), channel_id=1, source_target_pairs={{0,2},{1,3},{2,0},{3,1},{4,6},{5,7},{6,4},{7,5},{8,10},{9,11},{10,... | collective-permute-start | bytes 626696 | tf_op jit(solution)/shard_map/ppermute | solution.py:191
  6.3 1.5 %collective-permute-start.1 = (bf16[136,768]{1,0:T(8,128)(2,1)}, bf16[136,768]{1,0:T(8,128)(2,1)S(1)}, u32[]{:S(2)}, u32[]{:S(2)}) collective-permute-start(bf16[136,768]{1,0:T(8,128)(2,1)} %embed.1.refs_0_.refs_3_), channel_id=1, source_target_pairs={{0,4},{1,5},{2,6},{3,7},{4,0},{5,1},{6,2},{7,3},{8,12},{9,13},{10,... | collective-permute-start | bytes 626696 | tf_op jit(solution)/shard_map/ppermute | solution.py:191
  7.8 1.6 %collective-permute-start.2 = (bf16[136,768]{1,0:T(8,128)(2,1)}, bf16[136,768]{1,0:T(8,128)(2,1)S(1)}, u32[]{:S(2)}, u32[]{:S(2)}) collective-permute-start(bf16[136,768]{1,0:T(8,128)(2,1)} %embed.1.refs_0_.refs_3_), channel_id=1, source_target_pairs={{0,8},{1,9},{2,10},{3,11},{4,12},{5,13},{6,14},{7,15},{8,16},{9,17... | collective-permute-start | bytes 626696 | tf_op jit(solution)/shard_map/ppermute | solution.py:187
  9.4 1.6 %collective-permute-start.4 = (bf16[136,768]{1,0:T(8,128)(2,1)}, bf16[136,768]{1,0:T(8,128)(2,1)S(1)}, u32[]{:S(2)}, u32[]{:S(2)}) collective-permute-start(bf16[136,768]{1,0:T(8,128)(2,1)} %embed.1.refs_0_.refs_3_), channel_id=1, source_target_pairs={{16,0},{17,1},{18,2},{19,3},{20,4},{21,5},{22,6},{23,7},{8,24},{9,... | collective-permute-start | bytes 626696 | tf_op jit(solution)/shard_map/ppermute | solution.py:187
  11.0 0.7 %collective-permute-done.refs_1_ = bf16[136,768]{1,0:T(8,128)(2,1)S(1)} collective-permute-done((bf16[136,768]{1,0:T(8,128)(2,1)}, bf16[136,768]{1,0:T(8,128)(2,1)S(1)}, u32[]{:S(2)}, u32[]{:S(2)}) %collective-permute-start) | collective-permute-done | bytes 208928 | tf_op jit(solution)/shard_map/ppermute | solution.py:191
  11.7 1.8 %collective-permute-start.3 = (bf16[136,768]{1,0:T(8,128)(2,1)S(1)}, bf16[136,768]{1,0:T(8,128)(2,1)S(1)}, u32[]{:S(2)}, u32[]{:S(2)}) collective-permute-start(bf16[136,768]{1,0:T(8,128)(2,1)S(1)} %collective-permute-done.refs_1_), channel_id=1, source_target_pairs={{0,4},{1,5},{2,6},{3,7},{4,0},{5,1},{6,2},{7,3},{8,12},{9,13},{10,... | collective-permute-start | bytes 626696 | tf_op jit(solution)/shard_map/ppermute | solution.py:191
  13.5 4.5 %collective-permute-done.2.refs_4_.refs_5_ = bf16[136,768]{1,0:T(8,128)(2,1)S(1)} collective-permute-done((bf16[136,768]{1,0:T(8,128)(2,1)}, bf16[136,768]{1,0:T(8,128)(2,1)S(1)}, u32[]{:S(2)}, u32[]{:S(2)}) %collective-permute-start.2) | collective-permute-done | bytes 208928 | tf_op jit(solution)/shard_map/ppermute | solution.py:187
  18.0 2.8 %collective-permute-done.4.refs_6_ = bf16[136,768]{1,0:T(8,128)(2,1)S(1)} collective-permute-done((bf16[136,768]{1,0:T(8,128)(2,1)}, bf16[136,768]{1,0:T(8,128)(2,1)S(1)}, u32[]{:S(2)}, u32[]{:S(2)}) %collective-permute-start.4) | collective-permute-done | bytes 208928 | tf_op jit(solution)/shard_map/ppermute | solution.py:187
  20.8 0.0 collective-permute-start.7
  20.8 0.9 %copy-done = bf16[136,768]{1,0:T(8,128)(2,1)S(1)} copy-done((bf16[136,768]{1,0:T(8,128)(2,1)S(1)}, bf16[136,768]{1,0:T(8,128)(2,1)}, u32[]{:S(2)}) %copy-start) | copy-done | bytes 208920
  21.7 0.5 %score_soon.1 = (f32[2,128]{1,0:T(2,128)S(1)}, f32[4,128]{1,0:T(4,128)S(1)}, bf16[136,768]{1,0:T(8,128)(2,1)S(1)}) custom-call(bf16[136,768]{1,0:T(8,128)(2,1)S(1)} %copy-done, bf16[136,768]{1,0:T(8,128)(2,1)S(1)} %collective-permute-done.refs_1_, bf16[136,768]{1,0:T(8,128)(2,1)S(1)} %collective-permute-done.1.refs_2_, bf16[136,768]{1,0:T(8,128)(2,1)S(1)} %copy-done, ...), custom_call_target="tpu_custom_call" | custom-call | flops 150994944 | bytes 983040 | tf_op jit(solution)/shard_map/score_soon/pallas_call | solution.py:155
  22.3 0.6 %score_late.1 = (f32[3,128]{1,0:T(4,128)S(1)}, f32[4,128]{1,0:T(4,128)S(1)}) custom-call(bf16[136,768]{1,0:T(8,128)(2,1)S(1)} %get-tuple-element.14.refs_0_.refs_4_, bf16[136,768]{1,0:T(8,128)(2,1)S(1)} %collective-permute-done.refs_1_, bf16[136,768]{1,0:T(8,128)(2,1)S(1)} %collective-permute-done.1.refs_2_, ...), custom_call_target="tpu_custom_call" | custom-call | flops 150994944 | bytes 1376256 | tf_op jit(solution)/shard_map/score_late/pallas_call | solution.py:155
  22.9 0.8 %score_partner.1 = (f32[3,128]{1,0:T(4,128)S(1)}, f32[2,128]{1,0:T(2,128)S(1)}, f32[2,128]{1,0:T(2,128)S(1)}) custom-call(bf16[136,768]{1,0:T(8,128)(2,1)S(1)} %get-tuple-element.14.refs_0_.refs_4_, bf16[136,768]{1,0:T(8,128)(2,1)S(1)} %collective-permute-done.refs_1_, bf16[136,768]{1,0:T(8,128)(2,1)S(1)} %collective-permute-done.1.refs_2_, ...), custom_call_target="tpu_custom_call" | custom-call | flops 301989888 | bytes 1376256 | tf_op jit(solution)/shard_map/score_partner/pallas_call | solution.py:155
  23.7 0.5 %collective-permute-start.8 = (f32[3,128]{1,0:T(4,128)S(1)}, f32[3,128]{1,0:T(4,128)S(1)}, u32[]{:S(2)}, u32[]{:S(2)}) collective-permute-start(f32[3,128]{1,0:T(4,128)S(1)} %get-tuple-element.20), channel_id=1, source_target_pairs={{0,1},{1,0},{2,3},{3,2},{4,5},{5,4},{6,7},{7,6},{8,9},{9,8},{10,11... | collective-permute-start | bytes 4616 | tf_op jit(solution)/shard_map/ppermute | solution.py:191
  24.2 0.5 %collective-permute-start.11 = (f32[2,128]{1,0:T(2,128)S(1)}, f32[2,128]{1,0:T(2,128)S(1)}, u32[]{:S(2)}, u32[]{:S(2)}) collective-permute-start(f32[2,128]{1,0:T(2,128)S(1)} %get-tuple-element.22), channel_id=1, source_target_pairs={{0,4},{1,5},{2,6},{3,7},{4,0},{5,1},{6,2},{7,3},{8,12},{9,13},{10,... | collective-permute-start | bytes 3080 | tf_op jit(solution)/shard_map/ppermute | solution.py:191
  24.7 0.3 collective-permute-done.8
  25.0 2.1 %collective-permute-start.10 = (f32[1,128]{1,0:T(1,128)S(1)}, f32[1,128]{1,0:T(1,128)S(1)}, u32[]{:S(2)}, u32[]{:S(2)}) collective-permute-start(f32[1,128]{1,0:T(1,128)S(1)} %get-tuple-element.24), channel_id=1, source_target_pairs={{8,0},{9,1},{10,2},{11,3},{12,4},{13,5},{14,6},{15,7},{16,8},{17,9... | collective-permute-start | bytes 1544 | tf_op jit(solution)/shard_map/ppermute | solution.py:187
  27.1 0.7 %collective-permute-done.11 = f32[2,128]{1,0:T(2,128)S(1)} collective-permute-done((f32[2,128]{1,0:T(2,128)S(1)}, f32[2,128]{1,0:T(2,128)S(1)}, u32[]{:S(2)}, u32[]{:S(2)}) %collective-permute-start.11) | collective-permute-done | bytes 1056 | tf_op jit(solution)/shard_map/ppermute | solution.py:191
  27.8 0.5 %collective-permute-start.12 = (f32[1,128]{1,0:T(1,128)S(1)}, f32[1,128]{1,0:T(1,128)S(1)}, u32[]{:S(2)}, u32[]{:S(2)}) collective-permute-start(f32[1,128]{1,0:T(1,128)S(1)} %slice.19), channel_id=1, source_target_pairs={{0,2},{1,3},{2,0},{3,1},{4,6},{5,7},{6,4},{7,5},{8,10},{9,11},{10,... | collective-permute-start | bytes 1544 | tf_op jit(solution)/shard_map/ppermute | solution.py:191
  28.3 0.3 collective-permute-done.10
  28.6 2.1 %collective-permute-done.9 = f32[1,128]{1,0:T(1,128)S(1)} collective-permute-done((f32[1,128]{1,0:T(1,128)S(1)}, f32[1,128]{1,0:T(1,128)S(1)}, u32[]{:S(2)}, u32[]{:S(2)}) %collective-permute-start.9) | collective-permute-done | bytes 544 | tf_op jit(solution)/shard_map/ppermute | solution.py:187
  30.6 0.7 %collective-permute-done.12 = f32[1,128]{1,0:T(1,128)S(1)} collective-permute-done((f32[1,128]{1,0:T(1,128)S(1)}, f32[1,128]{1,0:T(1,128)S(1)}, u32[]{:S(2)}, u32[]{:S(2)}) %collective-permute-start.12) | collective-permute-done | bytes 544 | tf_op jit(solution)/shard_map/ppermute | solution.py:191
  31.3 0.5 %maximum_bitcast_fusion = f32[128]{0:T(128)} fusion(f32[1,128]{1,0:T(1,128)S(1)} %collective-permute-done.12, f32[1,128]{1,0:T(1,128)S(1)} %maximum_maximum_fusion, f32[2,128]{1,0:T(2,128)S(1)} %max.21), kind=kLoop, calls=%fused_computation | loop fusion | flops 256 | bytes 2048 | tf_op jit(solution)/shard_map/reshape | solution.py:234
  (14 shorter events, 0.0 us)
Async XLA Ops:
  3.3 8.4 %collective-permute-start = (bf16[136,768]{1,0:T(8,128)(2,1)}, bf16[136,768]{1,0:T(8,128)(2,1)S(1)}, u32[]{:S(2)}, u32[]{:S(2)}) collective-permute-start(bf16[136,768]{1,0:T(8,128)(2,1)} %embed.1.refs_0_.refs_3_), channel_id=1, source_target_pairs={{0,2},{1,3},{2,0},{3,1},{4,6},{5,7},{6,4},{7,5},{8,10},{9,11},{10,... | collective-permute-start | bytes 626696 | tf_op jit(solution)/shard_map/ppermute | solution.py:191
  6.3 7.1 %collective-permute-start.1 = (bf16[136,768]{1,0:T(8,128)(2,1)}, bf16[136,768]{1,0:T(8,128)(2,1)S(1)}, u32[]{:S(2)}, u32[]{:S(2)}) collective-permute-start(bf16[136,768]{1,0:T(8,128)(2,1)} %embed.1.refs_0_.refs_3_), channel_id=1, source_target_pairs={{0,4},{1,5},{2,6},{3,7},{4,0},{5,1},{6,2},{7,3},{8,12},{9,13},{10,... | collective-permute-start | bytes 626696 | tf_op jit(solution)/shard_map/ppermute | solution.py:191
  7.8 10.2 %collective-permute-start.2 = (bf16[136,768]{1,0:T(8,128)(2,1)}, bf16[136,768]{1,0:T(8,128)(2,1)S(1)}, u32[]{:S(2)}, u32[]{:S(2)}) collective-permute-start(bf16[136,768]{1,0:T(8,128)(2,1)} %embed.1.refs_0_.refs_3_), channel_id=1, source_target_pairs={{0,8},{1,9},{2,10},{3,11},{4,12},{5,13},{6,14},{7,15},{8,16},{9,17... | collective-permute-start | bytes 626696 | tf_op jit(solution)/shard_map/ppermute | solution.py:187
  9.4 11.3 %collective-permute-start.4 = (bf16[136,768]{1,0:T(8,128)(2,1)}, bf16[136,768]{1,0:T(8,128)(2,1)S(1)}, u32[]{:S(2)}, u32[]{:S(2)}) collective-permute-start(bf16[136,768]{1,0:T(8,128)(2,1)} %embed.1.refs_0_.refs_3_), channel_id=1, source_target_pairs={{16,0},{17,1},{18,2},{19,3},{20,4},{21,5},{22,6},{23,7},{8,24},{9,... | collective-permute-start | bytes 626696 | tf_op jit(solution)/shard_map/ppermute | solution.py:187
  11.7 10.6 %collective-permute-start.3 = (bf16[136,768]{1,0:T(8,128)(2,1)S(1)}, bf16[136,768]{1,0:T(8,128)(2,1)S(1)}, u32[]{:S(2)}, u32[]{:S(2)}) collective-permute-start(bf16[136,768]{1,0:T(8,128)(2,1)S(1)} %collective-permute-done.refs_1_), channel_id=1, source_target_pairs={{0,4},{1,5},{2,6},{3,7},{4,0},{5,1},{6,2},{7,3},{8,12},{9,13},{10,... | collective-permute-start | bytes 626696 | tf_op jit(solution)/shard_map/ppermute | solution.py:191
  13.5 9.4 %collective-permute-start.5 = (bf16[136,768]{1,0:T(8,128)(2,1)}, bf16[136,768]{1,0:T(8,128)(2,1)S(1)}, u32[]{:S(2)}, u32[]{:S(2)}) collective-permute-start(bf16[136,768]{1,0:T(8,128)(2,1)} %embed.1.refs_0_.refs_3_), channel_id=1, source_target_pairs={{0,1},{1,0},{2,3},{3,2},{4,5},{5,4},{6,7},{7,6},{8,9},{9,8},{10,11... | collective-permute-start | bytes 626696 | tf_op jit(solution)/shard_map/ppermute | solution.py:191
  18.0 4.9 %collective-permute-start.6 = (bf16[136,768]{1,0:T(8,128)(2,1)S(1)}, bf16[136,768]{1,0:T(8,128)(2,1)S(1)}, u32[]{:S(2)}, u32[]{:S(2)}) collective-permute-start(bf16[136,768]{1,0:T(8,128)(2,1)S(1)} %collective-permute-done.2.refs_4_.refs_5_), channel_id=1, source_target_pairs={{0,1},{1,0},{2,3},{3,2},{4,5},{5,4},{6,7},{7,6},{8,9},{9,8},{10,11... | collective-permute-start | bytes 626696 | tf_op jit(solution)/shard_map/ppermute | solution.py:191
  20.8 2.1 %collective-permute-start.7 = (bf16[136,768]{1,0:T(8,128)(2,1)S(1)}, bf16[136,768]{1,0:T(8,128)(2,1)S(1)}, u32[]{:S(2)}, u32[]{:S(2)}) collective-permute-start(bf16[136,768]{1,0:T(8,128)(2,1)S(1)} %collective-permute-done.4.refs_6_), channel_id=1, source_target_pairs={{0,1},{1,0},{2,3},{3,2},{4,5},{5,4},{6,7},{7,6},{8,9},{9,8},{10,11... | collective-permute-start | bytes 626696 | tf_op jit(solution)/shard_map/ppermute | solution.py:191
  20.8 0.9 %copy-start = (bf16[136,768]{1,0:T(8,128)(2,1)S(1)}, bf16[136,768]{1,0:T(8,128)(2,1)}, u32[]{:S(2)}) copy-start(bf16[136,768]{1,0:T(8,128)(2,1)} %embed.1.refs_0_.refs_3_) | copy-start | bytes 626692
  23.7 1.4 %collective-permute-start.8 = (f32[3,128]{1,0:T(4,128)S(1)}, f32[3,128]{1,0:T(4,128)S(1)}, u32[]{:S(2)}, u32[]{:S(2)}) collective-permute-start(f32[3,128]{1,0:T(4,128)S(1)} %get-tuple-element.20), channel_id=1, source_target_pairs={{0,1},{1,0},{2,3},{3,2},{4,5},{5,4},{6,7},{7,6},{8,9},{9,8},{10,11... | collective-permute-start | bytes 4616 | tf_op jit(solution)/shard_map/ppermute | solution.py:191
  24.2 3.6 %collective-permute-start.11 = (f32[2,128]{1,0:T(2,128)S(1)}, f32[2,128]{1,0:T(2,128)S(1)}, u32[]{:S(2)}, u32[]{:S(2)}) collective-permute-start(f32[2,128]{1,0:T(2,128)S(1)} %get-tuple-element.22), channel_id=1, source_target_pairs={{0,4},{1,5},{2,6},{3,7},{4,0},{5,1},{6,2},{7,3},{8,12},{9,13},{10,... | collective-permute-start | bytes 3080 | tf_op jit(solution)/shard_map/ppermute | solution.py:191
  25.0 3.5 %collective-permute-start.10 = (f32[1,128]{1,0:T(1,128)S(1)}, f32[1,128]{1,0:T(1,128)S(1)}, u32[]{:S(2)}, u32[]{:S(2)}) collective-permute-start(f32[1,128]{1,0:T(1,128)S(1)} %get-tuple-element.24), channel_id=1, source_target_pairs={{8,0},{9,1},{10,2},{11,3},{12,4},{13,5},{14,6},{15,7},{16,8},{17,9... | collective-permute-start | bytes 1544 | tf_op jit(solution)/shard_map/ppermute | solution.py:187
  27.1 3.5 %collective-permute-start.9 = (f32[1,128]{1,0:T(1,128)S(1)}, f32[1,128]{1,0:T(1,128)S(1)}, u32[]{:S(2)}, u32[]{:S(2)}) collective-permute-start(f32[1,128]{1,0:T(1,128)S(1)} %get-tuple-element.23), channel_id=1, source_target_pairs={{0,16},{1,17},{2,18},{3,19},{4,20},{5,21},{6,22},{7,23},{24,8},{25... | collective-permute-start | bytes 1544 | tf_op jit(solution)/shard_map/ppermute | solution.py:187
  27.8 3.5 %collective-permute-start.12 = (f32[1,128]{1,0:T(1,128)S(1)}, f32[1,128]{1,0:T(1,128)S(1)}, u32[]{:S(2)}, u32[]{:S(2)}) collective-permute-start(f32[1,128]{1,0:T(1,128)S(1)} %slice.19), channel_id=1, source_target_pairs={{0,2},{1,3},{2,0},{3,1},{4,6},{5,7},{6,4},{7,5},{8,10},{9,11},{10,... | collective-permute-start | bytes 1544 | tf_op jit(solution)/shard_map/ppermute | solution.py:191

commit v3 on v2

--- a/solution.py
+++ b/solution.py
@@ -200,9 +200,7 @@
     moves = tournament(line)
     visitors = [move(block, pairs) for pairs in moves]
     bits = [1 << i for i in range(1, plane.bit_length() - 1)]
-    row_blocks = [block]
-    for bit in bits:
-        row_blocks += [swap(here, bit) for here in row_blocks]
+    row_blocks = [block] + [swap(block, step) for step in range(2, plane, 2)]
 
     lanes = [block] + visitors
     every, count = tuple(range(len(lanes))), len(row_blocks)
@@ -211,8 +209,9 @@
         "score_soon", row_blocks[:-1], lanes[:-1], [(most, every[:-1])], [(0, count)], hold=True
     )
     row_blocks[0] = held
-    order = lax.optimization_barrier((lanes[0], row_blocks[-2]))[0]
-    partner = [swap(lane, 1) for lane in [order] + visitors]
+    partner = [lax.optimization_barrier((block, visitors[0]))[0], *visitors]
+    partner[-1] = lax.optimization_barrier((partner[-1], held))[0]
+    partner = [swap(lane, 1) for lane in partner]
     lanes[0] = held
     products = [(last, every), (most, every[-1:])]
     lines, backs = score(

time: 32 us -> 32.5 us (1.016)
  starting transfers between devices: 13.1 us -> 14.2 us
  Pallas kernels: 5.23 us -> 6.24 us
  local copies, waits for them, and re-layouts: 0.94 us -> 0.01 us
  waiting for transfers between devices: 12 us -> 11.3 us
    ppermute x4, waiting for transfers between devices: 9.6 us -> 5.09 us  [move(): return lax.ppermute(array, AXES, whole)]
    ppermute x9, waiting for transfers between devices: 2.4 us -> 6.23 us  [swap(): return lax.ppermute(array, AXES, pairs)]
    ppermute x4, starting transfers between devices: 5.21 us -> 7.75 us  [move(): return lax.ppermute(array, AXES, whole)]
    ppermute x9, starting transfers between devices: 7.89 us -> 6.48 us  [swap(): return lax.ppermute(array, AXES, pairs)]
    pallas_call x3, Pallas kernels: 1.92 us -> 2.95 us  [score(): pl.pallas_call(lambda *refs: score_kernel(*counts, *rest, *refs), in_spec...]
    unnamed x2 -> x0, local copies, waits for them, and re-layouts: 0.93 us -> none
  transfers between devices with their start and end apart: 13 -> 13, of which waited for: 8 -> 7; matrix products, arithmetic and copies ran while one was open for 0% -> 0% of each run, Pallas kernels for 4% -> 7%
where the time goes in v3:
time: 32.5 us; the launch traced here: 32.4 us
  starting transfers between devices  14.2 us (44%)
  waiting for transfers between devices  11.3 us (35%)
  Pallas kernels  6.24 us (19%)
  other arithmetic  0.52 us (2%)
    ppermute x4, starting transfers between devices, move(): return lax.ppermute(array, AXES, whole)  7.75 us
    ppermute x9, starting transfers between devices, swap(): return lax.ppermute(array, AXES, pairs)  6.48 us
    ppermute x9, waiting for transfers between devices, swap(): return lax.ppermute(array, AXES, pairs)  6.23 us
    ppermute x4, waiting for transfers between devices, move(): return lax.ppermute(array, AXES, whole)  5.09 us
    pallas_call x1, Pallas kernels, embed(): pl.pallas_call(embed_kernel, in_specs=[HBM] * 5, out_specs=VMEM, out_shap...  3.3 us
    pallas_call x3, Pallas kernels, score(): pl.pallas_call(lambda *refs: score_kernel(*counts, *rest, *refs), in_spec...  2.95 us
  transfers between devices with their start and end apart: 13, of which 7 were waited for; matrix products, arithmetic and copies ran while one was open for 0% of the time, Pallas kernels for 7%

profile of v3, /device:TPU:0, one launch (start us, length us, event | category | flops | bytes accessed | tf_op | source)
XLA Modules:
  0.0 32.4 jit_solution(15472351035774945303)
XLA Ops:
  0.0 3.3 %embed.1.refs_0_.refs_3_ = bf16[136,768]{1,0:T(8,128)(2,1)} custom-call(bf16[128,2048]{1,0:T(8,128)(2,1)} %states_hbm.1, bf16[2048,768]{1,0:T(8,128)(2,1)} %proj_hbm.1, s32[1,128]{1,0:T(1,128)} %bitcast.5, s32[1,128]{1,0:T(1,128)} %bitcast.6, s32[1,128]{1,0:T(1,128)} %bitcast.7), custom_call_target="tpu_custom_call" | custom-call | tf_op jit(solution)/shard_map/embed/pallas_call | solution.py:64
  3.3 3.1 %collective-permute-start.2 = (bf16[136,768]{1,0:T(8,128)(2,1)}, bf16[136,768]{1,0:T(8,128)(2,1)S(1)}, u32[]{:S(2)}, u32[]{:S(2)}) collective-permute-start(bf16[136,768]{1,0:T(8,128)(2,1)} %embed.1.refs_0_.refs_3_), channel_id=1, source_target_pairs={{0,8},{1,9},{2,10},{3,11},{4,12},{5,13},{6,14},{7,15},{8,16},{9,17... | collective-permute-start | bytes 626696 | tf_op jit(solution)/shard_map/ppermute | solution.py:187
  6.4 1.5 %collective-permute-start = (bf16[136,768]{1,0:T(8,128)(2,1)}, bf16[136,768]{1,0:T(8,128)(2,1)S(1)}, u32[]{:S(2)}, u32[]{:S(2)}) collective-permute-start(bf16[136,768]{1,0:T(8,128)(2,1)} %embed.1.refs_0_.refs_3_), channel_id=1, source_target_pairs={{0,2},{1,3},{2,0},{3,1},{4,6},{5,7},{6,4},{7,5},{8,10},{9,11},{10,... | collective-permute-start | bytes 626696 | tf_op jit(solution)/shard_map/ppermute | solution.py:191
  7.9 1.5 %collective-permute-start.1 = (bf16[136,768]{1,0:T(8,128)(2,1)}, bf16[136,768]{1,0:T(8,128)(2,1)S(1)}, u32[]{:S(2)}, u32[]{:S(2)}) collective-permute-start(bf16[136,768]{1,0:T(8,128)(2,1)} %embed.1.refs_0_.refs_3_), channel_id=1, source_target_pairs={{0,4},{1,5},{2,6},{3,7},{4,0},{5,1},{6,2},{7,3},{8,12},{9,13},{10,... | collective-permute-start | bytes 626696 | tf_op jit(solution)/shard_map/ppermute | solution.py:191
  9.4 1.6 %collective-permute-start.4 = (bf16[136,768]{1,0:T(8,128)(2,1)}, bf16[136,768]{1,0:T(8,128)(2,1)S(1)}, u32[]{:S(2)}, u32[]{:S(2)}) collective-permute-start(bf16[136,768]{1,0:T(8,128)(2,1)} %embed.1.refs_0_.refs_3_), channel_id=1, source_target_pairs={{16,0},{17,1},{18,2},{19,3},{20,4},{21,5},{22,6},{23,7},{8,24},{9,... | collective-permute-start | bytes 626696 | tf_op jit(solution)/shard_map/ppermute | solution.py:187
  11.0 0.5 %collective-permute-start.3 = (bf16[136,768]{1,0:T(8,128)(2,1)}, bf16[136,768]{1,0:T(8,128)(2,1)S(1)}, u32[]{:S(2)}, u32[]{:S(2)}) collective-permute-start(bf16[136,768]{1,0:T(8,128)(2,1)} %embed.1.refs_0_.refs_3_), channel_id=1, source_target_pairs={{0,6},{1,7},{2,4},{3,5},{4,2},{5,3},{6,0},{7,1},{8,14},{9,15},{10,... | collective-permute-start | bytes 626696 | tf_op jit(solution)/shard_map/ppermute | solution.py:191
  11.5 2.8 %collective-permute-done.2.refs_4_.refs_5_ = bf16[136,768]{1,0:T(8,128)(2,1)S(1)} collective-permute-done((bf16[136,768]{1,0:T(8,128)(2,1)}, bf16[136,768]{1,0:T(8,128)(2,1)S(1)}, u32[]{:S(2)}, u32[]{:S(2)}) %collective-permute-start.2) | collective-permute-done | bytes 208928 | tf_op jit(solution)/shard_map/ppermute | solution.py:187
  14.3 4.6 %collective-permute-done.1.refs_2_ = bf16[136,768]{1,0:T(8,128)(2,1)S(1)} collective-permute-done((bf16[136,768]{1,0:T(8,128)(2,1)}, bf16[136,768]{1,0:T(8,128)(2,1)S(1)}, u32[]{:S(2)}, u32[]{:S(2)}) %collective-permute-start.1) | collective-permute-done | bytes 208928 | tf_op jit(solution)/shard_map/ppermute | solution.py:191
  18.9 1.6 %score_soon.1 = (f32[2,128]{1,0:T(2,128)S(1)}, f32[4,128]{1,0:T(4,128)S(1)}, bf16[136,768]{1,0:T(8,128)(2,1)S(1)}) custom-call(bf16[136,768]{1,0:T(8,128)(2,1)} %embed.1.refs_0_.refs_3_, bf16[136,768]{1,0:T(8,128)(2,1)S(1)} %collective-permute-done.refs_1_, bf16[136,768]{1,0:T(8,128)(2,1)S(1)} %collective-permute-done.1.refs_2_, ...), custom_call_target="tpu_custom_call" | custom-call | flops 150994944 | bytes 983040 | tf_op jit(solution)/shard_map/score_soon/pallas_call | solution.py:155
  20.6 0.5 %collective-permute-start.5 = (bf16[136,768]{1,0:T(8,128)(2,1)}, bf16[136,768]{1,0:T(8,128)(2,1)S(1)}, u32[]{:S(2)}, u32[]{:S(2)}) collective-permute-start(bf16[136,768]{1,0:T(8,128)(2,1)} %embed.1.refs_0_.refs_3_), channel_id=1, source_target_pairs={{0,1},{1,0},{2,3},{3,2},{4,5},{5,4},{6,7},{7,6},{8,9},{9,8},{10,11... | collective-permute-start | bytes 626696 | tf_op jit(solution)/shard_map/ppermute | solution.py:191
  21.1 0.1 collective-permute-start.6
  21.1 0.6 %score_late.1 = (f32[3,128]{1,0:T(4,128)S(1)}, f32[4,128]{1,0:T(4,128)S(1)}) custom-call(bf16[136,768]{1,0:T(8,128)(2,1)S(1)} %get-tuple-element.15.refs_0_.refs_4_, bf16[136,768]{1,0:T(8,128)(2,1)S(1)} %collective-permute-done.refs_1_, bf16[136,768]{1,0:T(8,128)(2,1)S(1)} %collective-permute-done.1.refs_2_, ...), custom_call_target="tpu_custom_call" | custom-call | flops 150994944 | bytes 1376256 | tf_op jit(solution)/shard_map/score_late/pallas_call | solution.py:155
  21.7 0.3 collective-permute-done.7.refs_6_
  22.0 0.5 %collective-permute-done.5.refs_4_ = bf16[136,768]{1,0:T(8,128)(2,1)S(1)} collective-permute-done((bf16[136,768]{1,0:T(8,128)(2,1)}, bf16[136,768]{1,0:T(8,128)(2,1)S(1)}, u32[]{:S(2)}, u32[]{:S(2)}) %collective-permute-start.5) | collective-permute-done | bytes 208928 | tf_op jit(solution)/shard_map/ppermute | solution.py:191
  22.5 0.1 collective-permute-done.6.refs_5_
  22.6 0.7 %score_partner.1 = (f32[3,128]{1,0:T(4,128)S(1)}, f32[2,128]{1,0:T(2,128)S(1)}, f32[2,128]{1,0:T(2,128)S(1)}) custom-call(bf16[136,768]{1,0:T(8,128)(2,1)S(1)} %get-tuple-element.15.refs_0_.refs_4_, bf16[136,768]{1,0:T(8,128)(2,1)S(1)} %collective-permute-done.refs_1_, bf16[136,768]{1,0:T(8,128)(2,1)S(1)} %collective-permute-done.1.refs_2_, ...), custom_call_target="tpu_custom_call" | custom-call | flops 301989888 | bytes 1376256 | tf_op jit(solution)/shard_map/score_partner/pallas_call | solution.py:155
  23.4 0.3 collective-permute-start.8
  23.6 1.5 %collective-permute-start.11 = (f32[2,128]{1,0:T(2,128)S(1)}, f32[2,128]{1,0:T(2,128)S(1)}, u32[]{:S(2)}, u32[]{:S(2)}) collective-permute-start(f32[2,128]{1,0:T(2,128)S(1)} %get-tuple-element.24), channel_id=1, source_target_pairs={{0,4},{1,5},{2,6},{3,7},{4,0},{5,1},{6,2},{7,3},{8,12},{9,13},{10,... | collective-permute-start | bytes 3080 | tf_op jit(solution)/shard_map/ppermute | solution.py:191
  25.1 2.4 %collective-permute-start.10 = (f32[1,128]{1,0:T(1,128)S(1)}, f32[1,128]{1,0:T(1,128)S(1)}, u32[]{:S(2)}, u32[]{:S(2)}) collective-permute-start(f32[1,128]{1,0:T(1,128)S(1)} %get-tuple-element.26), channel_id=1, source_target_pairs={{8,0},{9,1},{10,2},{11,3},{12,4},{13,5},{14,6},{15,7},{16,8},{17,9... | collective-permute-start | bytes 1544 | tf_op jit(solution)/shard_map/ppermute | solution.py:187
  27.6 0.7 %collective-permute-start.9 = (f32[1,128]{1,0:T(1,128)S(1)}, f32[1,128]{1,0:T(1,128)S(1)}, u32[]{:S(2)}, u32[]{:S(2)}) collective-permute-start(f32[1,128]{1,0:T(1,128)S(1)} %get-tuple-element.25), channel_id=1, source_target_pairs={{0,16},{1,17},{2,18},{3,19},{4,20},{5,21},{6,22},{7,23},{24,8},{25... | collective-permute-start | bytes 1544 | tf_op jit(solution)/shard_map/ppermute | solution.py:187
  28.2 0.6 %collective-permute-start.12 = (f32[1,128]{1,0:T(1,128)S(1)}, f32[1,128]{1,0:T(1,128)S(1)}, u32[]{:S(2)}, u32[]{:S(2)}) collective-permute-start(f32[1,128]{1,0:T(1,128)S(1)} %slice.19), channel_id=1, source_target_pairs={{0,2},{1,3},{2,0},{3,1},{4,6},{5,7},{6,4},{7,5},{8,10},{9,11},{10,... | collective-permute-start | bytes 1544 | tf_op jit(solution)/shard_map/ppermute | solution.py:191
  28.9 2.2 %collective-permute-done.9 = f32[1,128]{1,0:T(1,128)S(1)} collective-permute-done((f32[1,128]{1,0:T(1,128)S(1)}, f32[1,128]{1,0:T(1,128)S(1)}, u32[]{:S(2)}, u32[]{:S(2)}) %collective-permute-start.9) | collective-permute-done | bytes 544 | tf_op jit(solution)/shard_map/ppermute | solution.py:187
  31.1 0.7 %collective-permute-done.12 = f32[1,128]{1,0:T(1,128)S(1)} collective-permute-done((f32[1,128]{1,0:T(1,128)S(1)}, f32[1,128]{1,0:T(1,128)S(1)}, u32[]{:S(2)}, u32[]{:S(2)}) %collective-permute-start.12) | collective-permute-done | bytes 544 | tf_op jit(solution)/shard_map/ppermute | solution.py:191
  31.9 0.5 %maximum_bitcast_fusion = f32[128]{0:T(128)} fusion(f32[1,128]{1,0:T(1,128)S(1)} %collective-permute-done.12, f32[1,128]{1,0:T(1,128)S(1)} %maximum_maximum_fusion, f32[2,128]{1,0:T(2,128)S(1)} %max.21), kind=kLoop, calls=%fused_computation | loop fusion | flops 256 | bytes 2048 | tf_op jit(solution)/shard_map/reshape | solution.py:233
  (12 shorter events, 0.1 us)
Async XLA Ops:
  3.3 11.0 %collective-permute-start.2 = (bf16[136,768]{1,0:T(8,128)(2,1)}, bf16[136,768]{1,0:T(8,128)(2,1)S(1)}, u32[]{:S(2)}, u32[]{:S(2)}) collective-permute-start(bf16[136,768]{1,0:T(8,128)(2,1)} %embed.1.refs_0_.refs_3_), channel_id=1, source_target_pairs={{0,8},{1,9},{2,10},{3,11},{4,12},{5,13},{6,14},{7,15},{8,16},{9,17... | collective-permute-start | bytes 626696 | tf_op jit(solution)/shard_map/ppermute | solution.py:187
  6.4 7.9 %collective-permute-start = (bf16[136,768]{1,0:T(8,128)(2,1)}, bf16[136,768]{1,0:T(8,128)(2,1)S(1)}, u32[]{:S(2)}, u32[]{:S(2)}) collective-permute-start(bf16[136,768]{1,0:T(8,128)(2,1)} %embed.1.refs_0_.refs_3_), channel_id=1, source_target_pairs={{0,2},{1,3},{2,0},{3,1},{4,6},{5,7},{6,4},{7,5},{8,10},{9,11},{10,... | collective-permute-start | bytes 626696 | tf_op jit(solution)/shard_map/ppermute | solution.py:191
  7.9 11.0 %collective-permute-start.1 = (bf16[136,768]{1,0:T(8,128)(2,1)}, bf16[136,768]{1,0:T(8,128)(2,1)S(1)}, u32[]{:S(2)}, u32[]{:S(2)}) collective-permute-start(bf16[136,768]{1,0:T(8,128)(2,1)} %embed.1.refs_0_.refs_3_), channel_id=1, source_target_pairs={{0,4},{1,5},{2,6},{3,7},{4,0},{5,1},{6,2},{7,3},{8,12},{9,13},{10,... | collective-permute-start | bytes 626696 | tf_op jit(solution)/shard_map/ppermute | solution.py:191
  9.4 11.1 %collective-permute-start.4 = (bf16[136,768]{1,0:T(8,128)(2,1)}, bf16[136,768]{1,0:T(8,128)(2,1)S(1)}, u32[]{:S(2)}, u32[]{:S(2)}) collective-permute-start(bf16[136,768]{1,0:T(8,128)(2,1)} %embed.1.refs_0_.refs_3_), channel_id=1, source_target_pairs={{16,0},{17,1},{18,2},{19,3},{20,4},{21,5},{22,6},{23,7},{8,24},{9,... | collective-permute-start | bytes 626696 | tf_op jit(solution)/shard_map/ppermute | solution.py:187
  11.0 10.2 %collective-permute-start.3 = (bf16[136,768]{1,0:T(8,128)(2,1)}, bf16[136,768]{1,0:T(8,128)(2,1)S(1)}, u32[]{:S(2)}, u32[]{:S(2)}) collective-permute-start(bf16[136,768]{1,0:T(8,128)(2,1)} %embed.1.refs_0_.refs_3_), channel_id=1, source_target_pairs={{0,6},{1,7},{2,4},{3,5},{4,2},{5,3},{6,0},{7,1},{8,14},{9,15},{10,... | collective-permute-start | bytes 626696 | tf_op jit(solution)/shard_map/ppermute | solution.py:191
  20.5 1.5 %collective-permute-start.7 = (bf16[136,768]{1,0:T(8,128)(2,1)S(1)}, bf16[136,768]{1,0:T(8,128)(2,1)S(1)}, u32[]{:S(2)}, u32[]{:S(2)}) collective-permute-start(bf16[136,768]{1,0:T(8,128)(2,1)S(1)} %collective-permute-done.4.refs_6_), channel_id=1, source_target_pairs={{0,1},{1,0},{2,3},{3,2},{4,5},{5,4},{6,7},{7,6},{8,9},{9,8},{10,11... | collective-permute-start | bytes 626696 | tf_op jit(solution)/shard_map/ppermute | solution.py:191
  20.6 2.0 %collective-permute-start.5 = (bf16[136,768]{1,0:T(8,128)(2,1)}, bf16[136,768]{1,0:T(8,128)(2,1)S(1)}, u32[]{:S(2)}, u32[]{:S(2)}) collective-permute-start(bf16[136,768]{1,0:T(8,128)(2,1)} %embed.1.refs_0_.refs_3_), channel_id=1, source_target_pairs={{0,1},{1,0},{2,3},{3,2},{4,5},{5,4},{6,7},{7,6},{8,9},{9,8},{10,11... | collective-permute-start | bytes 626696 | tf_op jit(solution)/shard_map/ppermute | solution.py:191
  21.1 1.5 %collective-permute-start.6 = (bf16[136,768]{1,0:T(8,128)(2,1)S(1)}, bf16[136,768]{1,0:T(8,128)(2,1)S(1)}, u32[]{:S(2)}, u32[]{:S(2)}) collective-permute-start(bf16[136,768]{1,0:T(8,128)(2,1)S(1)} %collective-permute-done.2.refs_4_.refs_5_), channel_id=1, source_target_pairs={{0,1},{1,0},{2,3},{3,2},{4,5},{5,4},{6,7},{7,6},{8,9},{9,8},{10,11... | collective-permute-start | bytes 626696 | tf_op jit(solution)/shard_map/ppermute | solution.py:191
  23.4 1.8 %collective-permute-start.8 = (f32[3,128]{1,0:T(4,128)S(1)}, f32[3,128]{1,0:T(4,128)S(1)}, u32[]{:S(2)}, u32[]{:S(2)}) collective-permute-start(f32[3,128]{1,0:T(4,128)S(1)} %get-tuple-element.22), channel_id=1, source_target_pairs={{0,1},{1,0},{2,3},{3,2},{4,5},{5,4},{6,7},{7,6},{8,9},{9,8},{10,11... | collective-permute-start | bytes 4616 | tf_op jit(solution)/shard_map/ppermute | solution.py:191
  23.6 4.6 %collective-permute-start.11 = (f32[2,128]{1,0:T(2,128)S(1)}, f32[2,128]{1,0:T(2,128)S(1)}, u32[]{:S(2)}, u32[]{:S(2)}) collective-permute-start(f32[2,128]{1,0:T(2,128)S(1)} %get-tuple-element.24), channel_id=1, source_target_pairs={{0,4},{1,5},{2,6},{3,7},{4,0},{5,1},{6,2},{7,3},{8,12},{9,13},{10,... | collective-permute-start | bytes 3080 | tf_op jit(solution)/shard_map/ppermute | solution.py:191
  25.1 3.7 %collective-permute-start.10 = (f32[1,128]{1,0:T(1,128)S(1)}, f32[1,128]{1,0:T(1,128)S(1)}, u32[]{:S(2)}, u32[]{:S(2)}) collective-permute-start(f32[1,128]{1,0:T(1,128)S(1)} %get-tuple-element.26), channel_id=1, source_target_pairs={{8,0},{9,1},{10,2},{11,3},{12,4},{13,5},{14,6},{15,7},{16,8},{17,9... | collective-permute-start | bytes 1544 | tf_op jit(solution)/shard_map/ppermute | solution.py:187
  27.6 3.5 %collective-permute-start.9 = (f32[1,128]{1,0:T(1,128)S(1)}, f32[1,128]{1,0:T(1,128)S(1)}, u32[]{:S(2)}, u32[]{:S(2)}) collective-permute-start(f32[1,128]{1,0:T(1,128)S(1)} %get-tuple-element.25), channel_id=1, source_target_pairs={{0,16},{1,17},{2,18},{3,19},{4,20},{5,21},{6,22},{7,23},{24,8},{25... | collective-permute-start | bytes 1544 | tf_op jit(solution)/shard_map/ppermute | solution.py:187
  28.2 3.6 %collective-permute-start.12 = (f32[1,128]{1,0:T(1,128)S(1)}, f32[1,128]{1,0:T(1,128)S(1)}, u32[]{:S(2)}, u32[]{:S(2)}) collective-permute-start(f32[1,128]{1,0:T(1,128)S(1)} %slice.19), channel_id=1, source_target_pairs={{0,2},{1,3},{2,0},{3,1},{4,6},{5,7},{6,4},{7,5},{8,10},{9,11},{10,... | collective-permute-start | bytes 1544 | tf_op jit(solution)/shard_map/ppermute | solution.py:191
